TPU v7x, 32 devices: a whole 2x2x4 slice. The times are simulated.
32 devices in a mesh: group: 2 (over y), dp: 4 (over z), tok: 4 (over x, core).
Axes of the slice: x: 2, y: 2, z: 4, core: 2. Of those that a mesh axis runs over, the one named last changes fastest.
Arguments:
- pre_norm: bfloat16 [384, 16, 1536], P(('group', 'dp'), 'tok'), parts along dimension 0, may hold values from -6 to 6
- cotangent: bfloat16 [384, 16, 1536], P(('group', 'dp'), 'tok'), parts along dimension 0, may hold values from -6 to 6
- gain: float32 [16, 1536], P('tok'), may hold values from 0.5 to 1.5
- pre_act: bfloat16 [384, 16, 6144], P('group', 'tok', 'dp'), parts along dimension 0, may hold values from -6 to 6
- gates: float32 [8, 16, 6144], P(None, 'tok', 'dp'), may hold values from 0.25 to 4
- down_weight: bfloat16 [16, 6144, 1536], P('tok', 'dp'), may hold values from -0.078125 to 0.078125
- scenario: int32 [384], P('group'), parts along dimension 0, may hold values from 0 to 7
Outputs:
- d_input: bfloat16 [384, 16, 1536], P(('group', 'dp'), 'tok'), parts along dimension 0
- d_pre_act: bfloat16 [384, 16, 6144], P('group', 'tok', 'dp'), parts along dimension 0
- d_down: bfloat16 [32, 6144, 1536], P(('group', 'tok'), 'dp'), parts along dimension 0
- d_gates: float32 [16, 16, 6144], P('group', 'tok', 'dp'), parts along dimension 0
- gain_gradient: float32 [32, 1536], P(('group', 'tok'), 'dp'), parts along dimension 0
There are 2 independent parts, one for each index of `group`. A program takes and returns all parts, laid end to end along the dimension named above; an argument that names none is the same for every part. Nothing has to cross between parts.
All inputs are finite; a program needn't handle non-finite values.
Results may differ from a plain program's by a relative error of at most 0.0058.
Values may be sent and summed in bfloat16 or wider, within the bound.
No kernel may reach another device: no remote copies, remote signals or barrier semaphores. Data moves between devices by JAX's collectives and lax.ppermute only.
A program may use at most 128 MiB of HBM per device.

v0:
```python
import jax
import jax.numpy as jnp
from jax import lax
from jax.sharding import PartitionSpec as P


def gelu_parts(value):
    cubic = 0.7978845608 * (value + 0.044715 * value * value * value)
    tangent = jnp.tanh(cubic)
    activated = 0.5 * value * (1.0 + tangent)
    slope = 0.5 * (1.0 + tangent) + 0.5 * value * (1.0 - tangent * tangent) * 0.7978845608 * (
        1.0 + 3.0 * 0.044715 * value * value
    )
    return (activated, slope)


def make_folder(pre_act, gates, down_weight, scenario):
    count = gates.shape[0]

    def folder(carry, piece, start):
        act = pre_act.astype(jnp.float32)
        onehot = (scenario[:, None] == jnp.arange(count, dtype=jnp.int32)[None, :]).astype(
            jnp.float32
        )
        gate_rows = jnp.einsum("bs,stf->btf", onehot, gates, precision=lax.Precision.HIGHEST)
        activated, slope = gelu_parts(act)
        hidden = (activated * gate_rows).astype(jnp.bfloat16)
        d_hidden = jnp.einsum(
            "btc,tfc->btf", piece, down_weight, preferred_element_type=jnp.float32
        )
        gate_acc = jnp.einsum(
            "bs,btf->stf", onehot, d_hidden * activated, precision=lax.Precision.HIGHEST
        )
        pre_rows = (d_hidden * gate_rows * slope).astype(jnp.bfloat16)
        down_acc = jnp.einsum("btf,btc->tfc", hidden, piece, preferred_element_type=jnp.float32)
        return (down_acc, gate_acc, pre_rows)

    return folder


def initial(pre_act, gates, down_weight):
    return (
        jnp.zeros(down_weight.shape, jnp.float32),
        jnp.zeros(gates.shape, jnp.float32),
        jnp.zeros(pre_act.shape, jnp.bfloat16),
    )


def per_device(pre_norm, cotangent, gain, pre_act, gates, down_weight, scenario):
    inputs = pre_norm.astype(jnp.float32)
    centered_rows = inputs - jnp.mean(inputs, axis=-1, keepdims=True)
    inverse_deviation = lax.rsqrt(
        jnp.mean(centered_rows * centered_rows, axis=-1, keepdims=True) + 1e-05
    )
    normalized_input = centered_rows * inverse_deviation
    gradient_results = cotangent.astype(jnp.float32)
    gain_gradient = lax.psum_scatter(
        jnp.sum(gradient_results * normalized_input, axis=0), "dp", scatter_dimension=1, tiled=True
    )
    scaled_gradient = gradient_results * gain
    norm_output_gradient = inverse_deviation * (
        scaled_gradient
        - jnp.mean(scaled_gradient, axis=-1, keepdims=True)
        - normalized_input * jnp.mean(scaled_gradient * normalized_input, axis=-1, keepdims=True)
    )
    dz_b = norm_output_gradient.astype(jnp.bfloat16)
    rows, local_toks, width = dz_b.shape
    all_toks = local_toks * lax.axis_size("tok")
    piece_width = width // all_toks
    folder = make_folder(pre_act, gates, down_weight, scenario)
    down_acc, gate_acc, pre_buf = folder(
        initial(pre_act, gates, down_weight),
        lax.all_gather(dz_b, "dp", axis=0, tiled=True),
        jnp.int32(0),
    )
    swapped = lax.all_to_all(dz_b, "tok", split_axis=2, concat_axis=1, tiled=True)
    mixed = (
        swapped.reshape(rows, all_toks, local_toks, piece_width)
        .transpose(0, 2, 1, 3)
        .reshape(rows, local_toks, width)
    )
    d_input = (dz_b.astype(jnp.float32) + mixed.astype(jnp.float32)).astype(jnp.bfloat16)
    return (d_input, pre_buf, down_acc.astype(jnp.bfloat16), gate_acc, gain_gradient)


def solution(mesh):
    placed = (
        P(("group", "dp"), "tok", None),
        P(("group", "dp"), "tok", None),
        P("tok", None),
        P("group", "tok", "dp"),
        P(None, "tok", "dp"),
        P("tok", "dp", None),
        P("group"),
    )
    return jax.shard_map(
        per_device,
        mesh=mesh,
        in_specs=placed,
        out_specs=(
            P(("group", "dp"), "tok", None),
            P("group", "tok", "dp"),
            P(("group", "tok"), "dp", None),
            P("group", "tok", "dp"),
            P(("group", "tok"), "dp"),
        ),
        check_vma=False,
    )
```

profile of v0, /device:TPU:0, one launch (start us, length us, event | category | flops | bytes accessed | tf_op | source)
XLA Modules:
  0.0 135.9 jit_solution(4278818894997703644)
XLA Ops:
  7.2 0.0 copy-start
  7.2 0.0 reduce-scatter.4.cloned.1.call-start
  7.2 1.3 convert_reduce_fusion
  8.5 1.4 %fusion.31 = f32[48,4]{0,1:T(4,128)S(1)} fusion(f32[48,4]{0,1:T(4,128)S(1)} %broadcast_multiply_fusion.2, bf16[48,4,1536]{2,1,0:T(4,128)(2,1)} %param.7), kind=kLoop, calls=%fused_computation.45 | loop fusion | flops 1179456 | bytes 591360 | tf_op jit(solution)/shard_map/reduce_sum | solution.py:53
  9.9 1.9 %fusion.33 = (f32[4,1536]{1,0:T(4,128)S(1)}, f32[48,4]{0,1:T(4,128)S(1)}, f32[48,4]{0,1:T(4,128)S(1)}) fusion(f32[48,4]{0,1:T(4,128)S(1)} %add_rsqrt_fusion, f32[48,4]{0,1:T(4,128)S(1)} %broadcast_multiply_fusion.2, bf16[48,4,1536]{2,1,0:T(4,128)(2,1)} %param.8, bf16[48,4,1536]{2,1,0:T(4,128)(2,1)} %param.7, f32[4,1536]{1,0:T(4,128)} %param.9), kind=kLoop, calls=%fused_computation.47 | loop fusion | flops 2942592 | bytes 1231872 | tf_op jit(solution)/shard_map/reduce_sum | solution.py:58
  11.8 1.2 copy.38
  13.0 0.0 reduce-scatter.4.cloned.1.call-update
  13.0 0.0 all-gather.2.cloned.1.call-start
  13.1 2.6 %fusion.30 = bf16[48,4,1536]{2,0,1:T(8,128)(2,1)} fusion(f32[48,4]{0,1:T(4,128)S(1)} %get-tuple-element.25, f32[48,4]{0,1:T(4,128)S(1)} %get-tuple-element.26, f32[4,1536]{1,0:T(4,128)} %param.9, f32[48,4]{0,1:T(4,128)S(1)} %add_rsqrt_fusion, f32[48,4]{0,1:T(4,128)S(1)} %broadcast_multiply_fusion.2, bf16[48,4,1536]{2,1,0:T(4,128)(2,1)} %param.8, ...), kind=kLoop, calls=%fused_computation.44 | loop fusion | flops 2949120 | bytes 1797120 | tf_op jit(solution)/shard_map/convert_element_type | solution.py:66
  15.6 0.0 all-gather.2.cloned.1.call-update
  15.7 2.5 %copy.30 = bf16[48,4,1536]{0,1,2:T(4,128)(2,1)S(1)} copy(bf16[48,4,1536]{2,0,1:T(8,128)(2,1)} %fusion.30) | data formatting | bytes 1179648 | tf_op jit(solution)/shard_map/convert_element_type | solution.py:66
  18.2 3.4 %reshape.45 = bf16[4,2,36864]{2,1,0:T(2,128)(2,1)} reshape(bf16[1536,4,48]{2,1,0:T(4,128)(2,1)S(1)} %bitcast.32) | data formatting | bytes 1179648
  21.6 4.2 %all-to-all-start = ((bf16[4,2,36864]{2,1,0:T(2,128)(2,1)}), bf16[4,2,36864]{2,1,0:T(2,128)(2,1)S(1)}, u32[]{:S(2)}, u32[]{:S(2)}) async-start(bf16[4,2,36864]{2,1,0:T(2,128)(2,1)} %reshape.45), calls=%async_computation | async-start | bytes 1179648 | tf_op jit(solution)/shard_map/all_to_all | solution.py:76
  25.8 13.4 %reduce-scatter.4.cloned.1.call-done = f32[384,4]{1,0:T(8,128)} async-done(((f32[1536,4]{1,0:T(8,128)}), f32[384,4]{1,0:T(8,128)}) %reduce-scatter.4.cloned.1.call-update) | async-done | bytes 6160
  39.2 1.6 %copy.39 = f32[4,384]{1,0:T(4,128)} copy(f32[4,384]{0,1:T(8,128)} %bitcast.36) | data formatting | bytes 12288
  40.8 0.0 all-to-all-done
  40.8 1.5 %reshape.46 = bf16[1536,4,48]{2,1,0:T(4,128)(2,1)S(1)} reshape(bf16[4,2,36864]{2,1,0:T(2,128)(2,1)S(1)} %all-to-all-done) | data formatting | bytes 1179648
  42.3 0.7 copy.31
  43.1 0.0 copy-start.3
  43.1 0.9 reshape.40
  44.0 2.1 %copy.32 = f32[48,4,16,96]{3,2,0,1:T(8,128)} copy(f32[48,4,16,96]{3,1,0,2:T(4,128)S(1)} %bitcast.31) | data formatting | bytes 2359296 | tf_op jit(solution)/shard_map/convert_element_type | solution.py:82
  46.0 2.1 %reshape.39 = f32[48,4,1536]{2,0,1:T(8,128)S(1)} reshape(f32[48,4,16,96]{3,2,0,1:T(8,128)} %copy.32) | data formatting | bytes 2359296 | tf_op jit(solution)/shard_map/convert_element_type | solution.py:82
  48.1 0.1 add_convert_fusion
  48.3 1.3 copy.35
  49.5 41.6 %all-gather.2.cloned.1.call-done = bf16[192,4,1536]{2,0,1:T(8,128)(2,1)} async-done(((bf16[48,4,1536]{2,0,1:T(8,128)(2,1)}), bf16[192,4,1536]{2,0,1:T(8,128)(2,1)}) %all-gather.2.cloned.1.call-update) | async-done | bytes 2359312 | tf_op jit(solution)/shard_map/all_gather | solution.py:73
  91.1 10.8 %fusion.49 = f32[4,192,1536]{2,1,0:T(8,128)S(1)} fusion(bf16[192,4,1536]{2,0,1:T(8,128)(2,1)} %all-gather.2.cloned.1.call-done, bf16[4,1536,1536]{2,1,0:T(8,128)(2,1)} %param.12), kind=kOutput, calls=%fused_computation.67 | convolution fusion | flops 3623878656 | bytes 25952256 | tf_op jit(solution)/shard_map/btc,tfc->btf/dot_general | solution.py:28
  101.9 3.4 %fusion.10 = f32[8,4,1536]{2,0,1:T(8,128)S(1)} fusion(f32[4,192,1536]{2,1,0:T(8,128)S(1)} %fusion.49, bf16[192,4,1536]{2,1,0:T(4,128)(2,1)S(1)} %copy-done.4, s32[192]{0:T(256)S(1)} %copy-done.5), kind=kOutput, calls=%fused_computation.20 | convolution fusion | flops 125044224 | bytes 7275264 | tf_op jit(solution)/shard_map/bs,btf->stf/dot_general | solution.py:31
  105.4 0.8 copy.37
  106.2 6.8 %fusion.6 = (bf16[192,4,1536]{2,0,1:T(8,128)(2,1)S(1)}, f32[192,4,1536]{2,0,1:T(8,128)}) fusion(f32[4,192,1536]{2,1,0:T(8,128)S(1)} %fusion.49, bf16[192,4,1536]{2,1,0:T(4,128)(2,1)S(1)} %copy-done.4, f32[8,4,1536]{2,1,0:T(4,128)S(1)} %copy-done, s32[192]{0:T(256)S(1)} %copy-done.5), kind=kOutput, calls=%fused_computation.14 | convolution fusion | flops 138020352 | bytes 14353152 | tf_op jit(solution)/shard_map/bs,stf->btf/dot_general | solution.py:25
  112.9 3.2 %copy.36 = bf16[192,4,1536]{2,1,0:T(4,128)(2,1)} copy(bf16[192,4,1536]{2,0,1:T(8,128)(2,1)S(1)} %get-tuple-element.23) | data formatting | bytes 4718592
  116.2 0.0 copy-done.2
  116.2 12.8 %convolution_convert_fusion = bf16[4,1536,1536]{2,1,0:T(8,128)(2,1)} fusion(bf16[192,4,1536]{2,0,1:T(8,128)(2,1)S(1)} %copy-done.2, f32[192,4,1536]{2,0,1:T(8,128)} %get-tuple-element.24, bf16[192,4,1536]{2,1,0:T(4,128)(2,1)S(1)} %copy-done.4), kind=kOutput, calls=%fused_computation | convolution fusion | flops 3646291968 | bytes 28311552 | tf_op jit(solution)/shard_map/btf,btc->tfc/dot_general | solution.py:35
  (12 shorter events, 0.0 us)
Async XLA Ops:
  7.2 99.0 %copy-start = (f32[8,4,1536]{2,1,0:T(4,128)S(1)}, f32[8,4,1536]{2,1,0:T(4,128)}, u32[]{:S(2)}) copy-start(f32[8,4,1536]{2,1,0:T(4,128)} %param.11) | copy-start | bytes 589828
  7.2 32.0 %reduce-scatter.4.cloned.1.call-start = ((), (), s32[]{:S(2)}) async-start(), calls=%async_computation.3 | async-start | bytes 983040
  13.0 78.1 %all-gather.2.cloned.1.call-start = ((), (), s32[]{:S(2)}) async-start(), calls=%async_computation.2 | async-start | bytes 2949120 | tf_op jit(solution)/shard_map/all_gather | solution.py:73
  21.6 19.2 %all-to-all-start = ((bf16[4,2,36864]{2,1,0:T(2,128)(2,1)}), bf16[4,2,36864]{2,1,0:T(2,128)(2,1)S(1)}, u32[]{:S(2)}, u32[]{:S(2)}) async-start(bf16[4,2,36864]{2,1,0:T(2,128)(2,1)} %reshape.45), calls=%async_computation | async-start | bytes 1179648 | tf_op jit(solution)/shard_map/all_to_all | solution.py:76
  43.1 5.1 %copy-start.3 = (bf16[48,4,1536]{2,0,1:T(8,128)(2,1)S(1)}, bf16[48,4,1536]{2,0,1:T(8,128)(2,1)}, u32[]{:S(2)}) copy-start(bf16[48,4,1536]{2,0,1:T(8,128)(2,1)} %fusion.30) | copy-start | bytes 1769476
  49.5 52.4 %copy-start.4 = (bf16[192,4,1536]{2,1,0:T(4,128)(2,1)S(1)}, bf16[192,4,1536]{2,1,0:T(4,128)(2,1)}, u32[]{:S(2)}) copy-start(bf16[192,4,1536]{2,1,0:T(4,128)(2,1)} %param.10) | copy-start | bytes 7077892
  49.5 52.4 %copy-start.5 = (s32[192]{0:T(256)S(1)}, s32[192]{0:T(256)}, u32[]{:S(2)}) copy-start(s32[192]{0:T(256)} %param.13) | copy-start | bytes 2308
  112.9 3.2 %copy-start.2 = (bf16[192,4,1536]{2,0,1:T(8,128)(2,1)S(1)}, bf16[192,4,1536]{2,0,1:T(8,128)(2,1)}, u32[]{:S(2)}) copy-start(bf16[192,4,1536]{2,0,1:T(8,128)(2,1)} %all-gather.2.cloned.1.call-done) | copy-start | bytes 7077892
  116.2 12.8 %copy-start.1 = (f32[8,4,1536]{2,1,0:T(4,128)S(1)}, f32[8,4,1536]{2,1,0:T(4,128)}, u32[]{:S(2)}) copy-start(f32[8,4,1536]{2,1,0:T(4,128)} %param.11) | copy-start | bytes 589828
Sparse Core Ops, SparseCore 0:
  13.2 25.9 reduce-scatter.3
  41.3 49.7 all-gather.1
where the time goes:
time: 136 us
  waiting for transfers between devices  55 us (40%)
  matrix products  33.8 us (25%)
  local copies, waits for them, and re-layouts  21.3 us (16%)
  between operations  14.1 us (10%)
  other arithmetic  7.26 us (5%)
  starting transfers between devices  4.29 us (3%)
    all_gather x1, waiting for transfers between devices, per_device(): lax.all_gather(dz_b, 'dp', axis=0, tiled=True)  41.6 us
    unnamed x3, waiting for transfers between devices  13.4 us
    unnamed x19, local copies, waits for them, and re-layouts  13.1 us
    dot_general x1, matrix products, folder(): jnp.einsum('btf,btc->tfc', hidden, piece, preferred_element_type=jnp.floa...  12.8 us
    dot_general x1, matrix products, folder(): jnp.einsum('btc,tfc->btf', piece, down_weight, preferred_element_type=jnp...  10.8 us
    dot_general x1, matrix products, folder(): jnp.einsum('bs,stf->btf', onehot, gates, precision=lax.Precision.HIGHEST)  6.76 us
    convert_element_type x4, local copies, waits for them, and re-layouts, per_device(): mixed.astype(jnp.float32)  5.74 us
    all_to_all x1, starting transfers between devices, per_device(): lax.all_to_all(dz_b, 'tok', split_axis=2, concat_axis=1, tiled=True)  4.21 us
  transfers between devices with their start and end apart: 3, of which 2 were waited for; matrix products, arithmetic and copies ran while one was open for 14% of the time, Pallas kernels for 0%

commit v1 on v0

v1 whole, which is shorter than its diff:
```python
import functools
import jax
import jax.numpy as jnp
import numpy as np
from jax import lax
from jax.experimental import pallas as pl
from jax.experimental.pallas import tpu as pltpu
from jax.sharding import PartitionSpec as P

F32 = jnp.float32
BF16 = jnp.bfloat16
MIB = 1 << 20


def gelu_parts(value):
    square = value * value
    tangent = jnp.tanh(0.7978845608 * (value + 0.044715 * value * square))
    half = 0.5 * (1.0 + tangent)
    activated = value * half
    slope = half + 0.5 * value * (1.0 - tangent * tangent) * 0.7978845608 * (
        1.0 + 3.0 * 0.044715 * square
    )
    return activated, slope


def ring_order(count):
    return [0] + list(range(1, count, 2)) + list(range(2, count, 2))[::-1]


def take_rows(rows_ref, t, count, toks):
    return jnp.concatenate(
        [rows_ref[j, pl.ds(t, count, stride=toks), :] for j in range(rows_ref.shape[0])], axis=1
    )


def put_rows(rows_ref, t, count, toks, value, first=0):
    for j in range(value.shape[1] // 128):
        rows_ref[first + j, pl.ds(t, count, stride=toks), :] = value[:, j * 128 : (j + 1) * 128]


def spill(rows_ref, out_ref):
    count, toks, width = out_ref.shape
    for j in range(width // 128):
        out_ref[:, :, j * 128 : (j + 1) * 128] = (
            rows_ref[j].reshape(count, toks, 128).astype(out_ref.dtype)
        )


def norm_kernel(x_ref, g_ref, gain_ref, dz_ref, send_ref, gg_ref, rows_ref):
    count, toks, width = x_ref.shape
    step = 8 // toks
    gain = jnp.concatenate([gain_ref[...]] * step, axis=0)
    scale = 1.0 / width
    total = jnp.zeros((8, width), F32)
    for i in range(count // step):
        x = x_ref[i * step : (i + 1) * step].astype(F32).reshape(8, width)
        ct = g_ref[i * step : (i + 1) * step].astype(F32).reshape(8, width)
        g = ct * gain
        c = x - jnp.sum(x, axis=-1, keepdims=True) * scale
        mean_g = jnp.sum(g, axis=-1, keepdims=True) * scale
        rstd = lax.rsqrt(jnp.sum(c * c, axis=-1, keepdims=True) * scale + 1e-05)
        mean_gc = jnp.sum(g * c, axis=-1, keepdims=True) * scale
        xhat = c * rstd
        total = total + ct * xhat
        dz = rstd * (g - mean_g - xhat * (mean_gc * rstd))
        for j in range(width // 128):
            rows_ref[j, i * 8 : (i + 1) * 8, :] = dz[:, j * 128 : (j + 1) * 128]
    part = sum(total[k * toks : (k + 1) * toks] for k in range(step))
    owners, _, share = gg_ref.shape
    for p in range(owners):
        gg_ref[p] = part[:, p * share : (p + 1) * share]
    groups = send_ref.shape[0]
    block = width // groups
    for t in range(toks):
        row = take_rows(rows_ref, t, count, toks).astype(BF16)
        dz_ref[t] = row
        for p in range(groups):
            send_ref[p, t] = row[:, p * block : (p + 1) * block]


def norm(pre_norm, cotangent, gain, owners, groups):
    count, toks, width = pre_norm.shape
    return pl.pallas_call(
        norm_kernel,
        out_shape=(
            jax.ShapeDtypeStruct((toks, count, width), BF16),
            jax.ShapeDtypeStruct((groups, toks, count, width // groups), BF16),
            jax.ShapeDtypeStruct((owners, toks, width // owners), F32),
        ),
        in_specs=[pl.BlockSpec(memory_space=pltpu.VMEM)] * 3,
        out_specs=[pl.BlockSpec(memory_space=pltpu.VMEM)] * 3,
        scratch_shapes=[pltpu.VMEM((width // 128, count * toks, 128), F32)],
        compiler_params=pltpu.CompilerParams(vmem_limit_bytes=16 * MIB),
        name="norm",
    )(pre_norm, cotangent, gain)


def mix_kernel(recv_ref, dz_ref, out_ref, rows_ref):
    groups, toks, count, block = recv_ref.shape
    piece = block // toks
    for q in range(groups):
        got = [recv_ref[q, i].astype(F32) for i in range(toks)]
        for j in range(toks):
            mixed = jnp.concatenate(
                [got[i][:, j * piece : (j + 1) * piece] for i in range(toks)], axis=1
            )
            mixed = mixed + dz_ref[j, :, q * block : (q + 1) * block].astype(F32)
            put_rows(rows_ref, j, count, toks, mixed, q * block // 128)
    spill(rows_ref, out_ref)


def mix(recv, dz):
    toks, count, width = dz.shape
    return pl.pallas_call(
        mix_kernel,
        out_shape=jax.ShapeDtypeStruct((count, toks, width), BF16),
        in_specs=[pl.BlockSpec(memory_space=pltpu.VMEM)] * 2,
        out_specs=pl.BlockSpec(memory_space=pltpu.VMEM),
        scratch_shapes=[pltpu.VMEM((width // 128, count * toks, 128), F32)],
        compiler_params=pltpu.CompilerParams(vmem_limit_bytes=16 * MIB),
        name="mix",
    )(recv, dz)


def act_kernel(pre_ref, gates_ref, hot_ref, ht_ref, act_ref, mul_ref, rows_ref):
    count, toks, width = pre_ref.shape
    scen = gates_ref.shape[0]
    for j in range(width // 128):
        rows_ref[j] = (
            pre_ref[:, :, j * 128 : (j + 1) * 128].astype(F32).reshape(count * toks, 128)
        )
    hot = hot_ref[...]
    for t in range(toks):
        gate = gates_ref[:, t, :]
        high = gate.astype(BF16)
        rest = gate - high.astype(F32)
        mid = rest.astype(BF16)
        low = (rest - mid.astype(F32)).astype(BF16)
        rate = (
            jnp.dot(hot, high, preferred_element_type=F32)
            + jnp.dot(hot, mid, preferred_element_type=F32)
            + jnp.dot(hot, low, preferred_element_type=F32)
        )
        activated, slope = gelu_parts(take_rows(rows_ref, t, count, toks))
        ht_ref[t] = (activated * rate).T.astype(BF16)
        act_ref[t] = activated
        mul_ref[t] = rate * slope


def activations(pre_act, gates, hot, block):
    count, toks, width = pre_act.shape
    scen = gates.shape[0]
    return pl.pallas_call(
        act_kernel,
        grid=(width // block,),
        in_specs=[
            pl.BlockSpec((count, toks, block), lambda i: (0, 0, i)),
            pl.BlockSpec((scen, toks, block), lambda i: (0, 0, i)),
            pl.BlockSpec((count, scen), lambda i: (0, 0)),
        ],
        out_specs=[
            pl.BlockSpec((toks, block, count), lambda i: (0, i, 0)),
            pl.BlockSpec((toks, count, block), lambda i: (0, 0, i)),
            pl.BlockSpec((toks, count, block), lambda i: (0, 0, i)),
        ],
        out_shape=(
            jax.ShapeDtypeStruct((toks, width, count), BF16),
            jax.ShapeDtypeStruct((toks, count, width), F32),
            jax.ShapeDtypeStruct((toks, count, width), F32),
        ),
        scratch_shapes=[pltpu.VMEM((block // 128, count * toks, 128), F32)],
        compiler_params=pltpu.CompilerParams(vmem_limit_bytes=24 * MIB),
        cost_estimate=pl.CostEstimate(
            flops=30 * count * toks * width,
            bytes_accessed=12 * count * toks * width,
            transcendentals=count * toks * width,
        ),
        name="act",
    )(pre_act, gates, hot)


def token_kernel(parts, earlier, merge, idx_ref, *refs):
    shards, refs = refs[:parts], refs[parts:]
    w_ref, act_ref, mul_ref, ht_ref, hot_ref = refs[:5]
    refs = refs[5:]
    if earlier:
        refs = refs[1:]
    done = ()
    if merge:
        done, refs = refs[: 2 * earlier], refs[2 * earlier :]
    down_ref, pre_ref, gate_ref = refs[:3]
    dz_ref = refs[3]

    @pl.when(pl.program_id(0) == 0)
    def _():
        size = shards[0].shape[0]
        for k in range(parts):
            start = pl.multiple_of(idx_ref[k] * size, 16)
            dz_ref[pl.ds(start, size), :] = shards[k][...]

    dz = dz_ref[...]
    d_hidden = lax.dot_general(
        dz, w_ref[0], (((1,), (1,)), ((), ())), preferred_element_type=F32
    )
    down_ref[0] = jnp.dot(ht_ref[0], dz, preferred_element_type=F32).astype(BF16)
    product = d_hidden * act_ref[0]
    high = product.astype(BF16)
    low = (product - high.astype(F32)).astype(BF16)
    hot = hot_ref[...]
    d_gate = jnp.dot(hot, high, preferred_element_type=F32) + jnp.dot(
        hot, low, preferred_element_type=F32
    )
    d_pre = d_hidden * mul_ref[0]
    if not merge:
        pre_ref[...] = d_pre.astype(BF16)
        gate_ref[...] = d_gate
    else:
        rows_ref = refs[4]
        count, toks, block = pre_ref.shape
        for t in range(earlier):
            put_rows(rows_ref, t, count, toks, done[2 * t][...].astype(F32))
            gate_ref[:, t, :] = done[2 * t + 1][...]
        put_rows(rows_ref, earlier, count, toks, d_pre)
        gate_ref[:, earlier, :] = d_gate
        spill(rows_ref, pre_ref)


def token_step(t, idx, shards, down_weight, act, mul, ht, hot_t, down, done, block):
    toks, hidden, width = down_weight.shape
    count = act.shape[1]
    scen = hot_t.shape[0]
    parts = len(shards)
    size = shards[0].shape[0]
    merge = t == toks - 1
    operands = list(shards) + [down_weight, act, mul, ht, hot_t]
    specs = [pl.BlockSpec((size, width), lambda i, s: (0, 0))] * parts + [
        pl.BlockSpec((1, block, width), lambda i, s: (t, i, 0)),
        pl.BlockSpec((1, count, block), lambda i, s: (t, 0, i)),
        pl.BlockSpec((1, count, block), lambda i, s: (t, 0, i)),
        pl.BlockSpec((1, block, count), lambda i, s: (t, i, 0)),
        pl.BlockSpec((scen, count), lambda i, s: (0, 0)),
    ]
    aliases = {}
    if t:
        aliases = {1 + len(operands): 0}
        operands.append(down)
        specs.append(pl.BlockSpec(memory_space=pl.ANY))
    scratch = [pltpu.VMEM((count, width), BF16)]
    if merge:
        for pre, gate in done:
            operands += [pre, gate]
            specs += [
                pl.BlockSpec((count, block), lambda i, s: (0, i)),
                pl.BlockSpec((scen, block), lambda i, s: (0, i)),
            ]
        scratch.append(pltpu.VMEM((block // 128, count * toks, 128), F32))
        pre_spec = pl.BlockSpec((count, toks, block), lambda i, s: (0, 0, i))
        gate_spec = pl.BlockSpec((scen, toks, block), lambda i, s: (0, 0, i))
        pre_shape, gate_shape = (count, toks, hidden), (scen, toks, hidden)
    else:
        pre_spec = pl.BlockSpec((count, block), lambda i, s: (0, i))
        gate_spec = pl.BlockSpec((scen, block), lambda i, s: (0, i))
        pre_shape, gate_shape = (count, hidden), (scen, hidden)
    return pl.pallas_call(
        functools.partial(token_kernel, parts, t, merge),
        grid_spec=pltpu.PrefetchScalarGridSpec(
            num_scalar_prefetch=1,
            grid=(hidden // block,),
            in_specs=specs,
            out_specs=[pl.BlockSpec((1, block, width), lambda i, s: (t, i, 0)), pre_spec, gate_spec],
            scratch_shapes=scratch,
        ),
        out_shape=(
            jax.ShapeDtypeStruct(down_weight.shape, BF16),
            jax.ShapeDtypeStruct(pre_shape, BF16),
            jax.ShapeDtypeStruct(gate_shape, F32),
        ),
        input_output_aliases=aliases,
        compiler_params=pltpu.CompilerParams(vmem_limit_bytes=24 * MIB),
        cost_estimate=pl.CostEstimate(
            flops=4 * count * hidden * width,
            bytes_accessed=4 * hidden * width + 12 * count * hidden,
            transcendentals=0,
        ),
        name="token",
    )(idx, *operands)


def plain_tokens(dz, pre_act, gates, down_weight, scenario):
    piece = lax.all_gather(dz, "dp", axis=1, tiled=True)
    onehot = (scenario[:, None] == jnp.arange(gates.shape[0], dtype=jnp.int32)[None, :]).astype(F32)
    rate = jnp.einsum("bs,stf->btf", onehot, gates, precision=lax.Precision.HIGHEST)
    activated, slope = gelu_parts(pre_act.astype(F32))
    hidden = (activated * rate).astype(BF16)
    d_hidden = jnp.einsum("tbc,tfc->btf", piece, down_weight, preferred_element_type=F32)
    gate = jnp.einsum("bs,btf->stf", onehot, d_hidden * activated, precision=lax.Precision.HIGHEST)
    pre = (d_hidden * rate * slope).astype(BF16)
    down = jnp.einsum("btf,tbc->tfc", hidden, piece, preferred_element_type=F32).astype(BF16)
    return pre, down, gate


def ring_tokens(dz, pre_act, gates, down_weight, scenario):
    dp = lax.axis_size("dp")
    toks = dz.shape[0]
    order = ring_order(dp)
    ring = [(order[k], order[(k + 1) % dp]) for k in range(dp)]
    sources = np.zeros((dp, dp), np.int32)
    for k in range(dp):
        for s in range(dp):
            sources[order[k], s] = order[(k - s) % dp]
    idx = lax.dynamic_index_in_dim(jnp.asarray(sources), lax.axis_index("dp"), 0, keepdims=False)

    shards = [[dz[t]] for t in range(toks)]
    for s in range(dp - 1):
        for t in range(toks):
            shards[t].append(lax.ppermute(shards[t][-1], "dp", ring))

    count = gates.shape[0]
    hot = (scenario[:, None] == jnp.arange(count, dtype=jnp.int32)[None, :]).astype(BF16)
    hot_t = (jnp.arange(count, dtype=jnp.int32)[:, None] == scenario[None, :]).astype(BF16)
    block = 256
    ht, act, mul = activations(pre_act, gates, hot, block)

    down, done = None, []
    for t in range(toks):
        down, pre, gate = token_step(
            t, idx, shards[t], down_weight, act, mul, ht, hot_t, down, done, block
        )
        done.append((pre, gate))
    return pre, down, gate


def per_device(pre_norm, cotangent, gain, pre_act, gates, down_weight, scenario):
    dp = lax.axis_size("dp")
    groups = lax.axis_size("tok")
    toks = pre_norm.shape[1]
    dz, send, gain_parts = norm(pre_norm, cotangent, gain, dp, groups)
    recv = lax.all_to_all(send, "tok", 0, 0, tiled=True)
    d_input = mix(recv, dz)
    gain_gradient = jnp.sum(lax.all_to_all(gain_parts, "dp", 0, 0, tiled=True), axis=0)

    if down_weight.shape[1] % 256:
        pre, down, gate = plain_tokens(dz, pre_act, gates, down_weight, scenario)
    else:
        pre, down, gate = ring_tokens(dz, pre_act, gates, down_weight, scenario)
    return (d_input, pre, down, gate, gain_gradient)


def solution(mesh):
    placed = (
        P(("group", "dp"), "tok", None),
        P(("group", "dp"), "tok", None),
        P("tok", None),
        P("group", "tok", "dp"),
        P(None, "tok", "dp"),
        P("tok", "dp", None),
        P("group"),
    )
    return jax.shard_map(
        per_device,
        mesh=mesh,
        in_specs=placed,
        out_specs=(
            P(("group", "dp"), "tok", None),
            P("group", "tok", "dp"),
            P(("group", "tok"), "dp", None),
            P("group", "tok", "dp"),
            P(("group", "tok"), "dp"),
        ),
        check_vma=False,
    )
```

time: 136 us -> 97.9 us (0.72)
  waiting for transfers between devices: 55 us -> 3.13 us
  Pallas kernels: 0 us -> 46.5 us
  matrix products: 33.8 us -> 0 us
  starting transfers between devices: 4.29 us -> 25.3 us
  between operations: 14.1 us -> 0.75 us
  other arithmetic: 7.26 us -> 2.06 us
  local copies, waits for them, and re-layouts: 21.3 us -> 18.9 us
    pallas_call x0 -> x7, Pallas kernels: none -> 46.5 us  [the longest x4 34.6 us: token_step(): pl.pallas_call(functools.partial(token_kernel, parts, t, merge), grid_spe...]
    all_gather x1 -> x0, waiting for transfers between devices: 41.6 us -> none  [per_device(): lax.all_gather(dz_b, 'dp', axis=0, tiled=True)]
    dot_general x4 -> x0, matrix products: 33.8 us -> none  [the longest x1 12.8 us: folder(): jnp.einsum('btf,btc->tfc', hidden, piece, preferred_element_type=jnp.floa...]
    ppermute x0 -> x12, starting transfers between devices: none -> 17.3 us  [ring_tokens(): shards[t].append(lax.ppermute(shards[t][-1], 'dp', ring))]
    unnamed x3 -> x0, waiting for transfers between devices: 13.4 us -> none
    convert_element_type x5 -> x0, local copies, waits for them, and re-layouts: 8.26 us -> none  [the longest x4 5.74 us: per_device(): mixed.astype(jnp.float32)]
    unnamed x19 -> x34, local copies, waits for them, and re-layouts: 13.1 us -> 18.1 us
    reduce_sum x3 -> x1, other arithmetic: 4.58 us -> 0.61 us  [per_device(): jnp.sum(lax.all_to_all(gain_parts, 'dp', 0, 0, tiled=True), axis=0)]
  transfers between devices with their start and end apart: 3 -> 14, of which waited for: 2 -> 3; matrix products, arithmetic and copies ran while one was open for 14% -> 3% of each run, Pallas kernels for 0% -> 36%
where the time goes in v1:
time: 97.9 us; the launch traced here: 96.6 us
  Pallas kernels  46.5 us (47%)
  starting transfers between devices  25.3 us (26%)
  local copies, waits for them, and re-layouts  18.9 us (19%)
  waiting for transfers between devices  3.13 us (3%)
  other arithmetic  2.06 us (2%)
    pallas_call x4, Pallas kernels, token_step(): pl.pallas_call(functools.partial(token_kernel, parts, t, merge), grid_spe...  34.6 us
    unnamed x34, local copies, waits for them, and re-layouts  18.1 us
    ppermute x12, starting transfers between devices, ring_tokens(): shards[t].append(lax.ppermute(shards[t][-1], 'dp', ring))  17.3 us
    pallas_call x1, Pallas kernels, activations(): pl.pallas_call(act_kernel, grid=(width // block,), in_specs=[pl.BlockSpec...  7.53 us
    all_to_all x1, starting transfers between devices, per_device(): recv = lax.all_to_all(send, 'tok', 0, 0, tiled=True)  4.16 us
    all_to_all x1, starting transfers between devices, per_device(): lax.all_to_all(gain_parts, 'dp', 0, 0, tiled=True)  3.86 us
    pallas_call x1, Pallas kernels, mix(): pl.pallas_call(mix_kernel, out_shape=jax.ShapeDtypeStruct((count, toks, w...  2.43 us
    ppermute x12, waiting for transfers between devices, ring_tokens(): shards[t].append(lax.ppermute(shards[t][-1], 'dp', ring))  2.38 us
  transfers between devices with their start and end apart: 14, of which 3 were waited for; matrix products, arithmetic and copies ran while one was open for 3% of the time, Pallas kernels for 36%

profile of v1, /device:TPU:0, one launch (start us, length us, event | category | flops | bytes accessed | tf_op | source)
XLA Modules:
  0.0 96.6 jit_solution(191263963882697065)
XLA Ops:
  0.6 1.1 %copy-done.11 = bf16[48,4,1536]{2,1,0:T(4,128)(2,1)S(1)} copy-done((bf16[48,4,1536]{2,1,0:T(4,128)(2,1)S(1)}, bf16[48,4,1536]{2,1,0:T(4,128)(2,1)}, u32[]{:S(2)}) %copy-start.11) | copy-done | bytes 589848
  1.7 1.1 %copy-done.12 = bf16[48,4,1536]{2,1,0:T(4,128)(2,1)S(1)} copy-done((bf16[48,4,1536]{2,1,0:T(4,128)(2,1)S(1)}, bf16[48,4,1536]{2,1,0:T(4,128)(2,1)}, u32[]{:S(2)}) %copy-start.12) | copy-done | bytes 589848
  3.5 1.9 %norm.1 = (bf16[4,48,1536]{2,1,0:T(8,128)(2,1)S(1)}, bf16[4,4,48,384]{3,2,1,0:T(8,128)(2,1)}, f32[4,4,384]{2,1,0:T(4,128)}) custom-call(bf16[48,4,1536]{2,1,0:T(4,128)(2,1)S(1)} %copy-done.11, bf16[48,4,1536]{2,1,0:T(4,128)(2,1)S(1)} %copy-done.12, f32[4,1536]{1,0:T(4,128)S(1)} %copy-done.16), custom_call_target="tpu_custom_call" | custom-call | tf_op jit(solution)/shard_map/norm/pallas_call | solution.py:83
  5.5 0.8 copy-done.4
  6.3 3.0 %collective-permute-start.9 = (bf16[48,1536]{1,0:T(8,128)(2,1)S(1)}, bf16[48,1536]{1,0:T(8,128)(2,1)S(1)}, u32[]{:S(2)}, u32[]{:S(2)}) collective-permute-start(bf16[48,1536]{1,0:T(8,128)(2,1)S(1)} %get-tuple-element.41.refs_0_), channel_id=1, source_target_pairs={{0,4},{4,12},{12,8},{8,0},{1,5},{5,13},{13,9},{9,1},{2,6},{6,14},{... | collective-permute-start | bytes 442376 | tf_op jit(solution)/shard_map/ppermute | solution.py:316
  9.3 3.9 %all-to-all-start.1 = ((f32[4,4,384]{2,1,0:T(4,128)}), f32[4,4,384]{2,1,0:T(4,128)S(1)}, u32[]{:S(2)}, u32[]{:S(2)}) async-start(f32[4,4,384]{2,1,0:T(4,128)} %get-tuple-element.40), calls=%async_computation.1 | async-start | bytes 49152 | tf_op jit(solution)/shard_map/all_to_all | solution.py:340
  13.2 2.0 %collective-permute-start.6 = (bf16[48,1536]{1,0:T(8,128)(2,1)S(1)}, bf16[48,1536]{1,0:T(8,128)(2,1)}, u32[]{:S(2)}, u32[]{:S(2)}) collective-permute-start(bf16[48,1536]{1,0:T(8,128)(2,1)S(1)} %get-tuple-element.42.refs_0_), channel_id=1, source_target_pairs={{0,4},{4,12},{12,8},{8,0},{1,5},{5,13},{13,9},{9,1},{2,6},{6,14},{... | collective-permute-start | bytes 442376 | tf_op jit(solution)/shard_map/ppermute | solution.py:316
  15.2 2.3 %collective-permute-start.3 = (bf16[48,1536]{1,0:T(8,128)(2,1)S(1)}, bf16[48,1536]{1,0:T(8,128)(2,1)}, u32[]{:S(2)}, u32[]{:S(2)}) collective-permute-start(bf16[48,1536]{1,0:T(8,128)(2,1)S(1)} %get-tuple-element.43.refs_0_), channel_id=1, source_target_pairs={{0,4},{4,12},{12,8},{8,0},{1,5},{5,13},{13,9},{9,1},{2,6},{6,14},{... | collective-permute-start | bytes 442376 | tf_op jit(solution)/shard_map/ppermute | solution.py:316
  18.2 0.8 all-to-all-done.1
  19.0 4.2 %all-to-all-start = ((bf16[4,4,48,384]{3,2,1,0:T(8,128)(2,1)}), bf16[4,4,48,384]{3,2,1,0:T(8,128)(2,1)}, u32[]{:S(2)}, u32[]{:S(2)}) async-start(bf16[4,4,48,384]{3,2,1,0:T(8,128)(2,1)} %get-tuple-element.23), calls=%async_computation | async-start | bytes 1179648 | tf_op jit(solution)/shard_map/all_to_all | solution.py:338
  23.1 0.8 fusion.hot_ref
  23.9 1.3 %collective-permute-start.7 = (bf16[48,1536]{1,0:T(8,128)(2,1)}, bf16[48,1536]{1,0:T(8,128)(2,1)}, u32[]{:S(2)}, u32[]{:S(2)}) collective-permute-start(bf16[48,1536]{1,0:T(8,128)(2,1)} %collective-permute-done.6.refs_1_), channel_id=1, source_target_pairs={{0,4},{4,12},{12,8},{8,0},{1,5},{5,13},{13,9},{9,1},{2,6},{6,14},{... | collective-permute-start | bytes 442376 | tf_op jit(solution)/shard_map/ppermute | solution.py:316
  25.2 2.3 %collective-permute-start.4 = (bf16[48,1536]{1,0:T(8,128)(2,1)}, bf16[48,1536]{1,0:T(8,128)(2,1)}, u32[]{:S(2)}, u32[]{:S(2)}) collective-permute-start(bf16[48,1536]{1,0:T(8,128)(2,1)} %collective-permute-done.3.refs_1_), channel_id=1, source_target_pairs={{0,4},{4,12},{12,8},{8,0},{1,5},{5,13},{13,9},{9,1},{2,6},{6,14},{... | collective-permute-start | bytes 442376 | tf_op jit(solution)/shard_map/ppermute | solution.py:316
  28.5 2.0 %collective-permute-done.10.refs_2_ = bf16[48,1536]{1,0:T(8,128)(2,1)} collective-permute-done((bf16[48,1536]{1,0:T(8,128)(2,1)S(1)}, bf16[48,1536]{1,0:T(8,128)(2,1)}, u32[]{:S(2)}, u32[]{:S(2)}) %collective-permute-start.10) | collective-permute-done | bytes 147488 | tf_op jit(solution)/shard_map/ppermute | solution.py:316
  30.6 1.0 %collective-permute-start.11 = (bf16[48,1536]{1,0:T(8,128)(2,1)}, bf16[48,1536]{1,0:T(8,128)(2,1)}, u32[]{:S(2)}, u32[]{:S(2)}) collective-permute-start(bf16[48,1536]{1,0:T(8,128)(2,1)} %collective-permute-done.10.refs_2_), channel_id=1, source_target_pairs={{0,4},{4,12},{12,8},{8,0},{1,5},{5,13},{13,9},{9,1},{2,6},{6,14},{... | collective-permute-start | bytes 442376 | tf_op jit(solution)/shard_map/ppermute | solution.py:316
  32.3 1.7 %copy-done.6 = bf16[192,4,1536]{2,1,0:T(4,128)(2,1)S(1)} copy-done((bf16[192,4,1536]{2,1,0:T(4,128)(2,1)S(1)}, bf16[192,4,1536]{2,1,0:T(4,128)(2,1)}, u32[]{:S(2)}) %copy-start.6) | copy-done | bytes 2359320
  34.0 0.9 copy-done.13
  34.9 7.5 %act.1 = (bf16[4,1536,192]{2,1,0:T(8,128)(2,1)S(1)}, f32[4,192,1536]{2,1,0:T(8,128)S(1)}, f32[4,192,1536]{2,1,0:T(8,128)S(1)}) custom-call(bf16[192,4,1536]{2,1,0:T(4,128)(2,1)S(1)} %copy-done.6, f32[8,4,1536]{2,1,0:T(4,128)S(1)} %copy-done.13, bf16[192,8]{1,0:T(8,128)(2,1)S(1)} %fusion.hot_ref), custom_call_target="tpu_custom_call" | custom-call | flops 35389440 | bytes 14155776 | tf_op jit(solution)/shard_map/act/pallas_call | solution.py:153
  42.4 2.2 %copy-done = f32[4,192,1536]{2,1,0:T(8,128)} copy-done((f32[4,192,1536]{2,1,0:T(8,128)}, f32[4,192,1536]{2,1,0:T(8,128)S(1)}, u32[]{:S(2)}) %copy-start) | copy-done | bytes 4718616
  44.6 2.1 %copy-done.2 = f32[4,192,1536]{2,1,0:T(8,128)} copy-done((f32[4,192,1536]{2,1,0:T(8,128)}, f32[4,192,1536]{2,1,0:T(8,128)S(1)}, u32[]{:S(2)}) %copy-start.2) | copy-done | bytes 4718616
  48.1 2.1 %collective-permute-start.8 = (bf16[48,1536]{1,0:T(8,128)(2,1)}, bf16[48,1536]{1,0:T(8,128)(2,1)}, u32[]{:S(2)}, u32[]{:S(2)}) collective-permute-start(bf16[48,1536]{1,0:T(8,128)(2,1)} %collective-permute-done.7.refs_2_), channel_id=1, source_target_pairs={{0,4},{4,12},{12,8},{8,0},{1,5},{5,13},{13,9},{9,1},{2,6},{6,14},{... | collective-permute-start | bytes 442376 | tf_op jit(solution)/shard_map/ppermute | solution.py:316
  50.5 1.5 %collective-permute-start.2 = (bf16[48,1536]{1,0:T(8,128)(2,1)}, bf16[48,1536]{1,0:T(8,128)(2,1)}, u32[]{:S(2)}, u32[]{:S(2)}) collective-permute-start(bf16[48,1536]{1,0:T(8,128)(2,1)} %collective-permute-done.1.refs_2_), channel_id=1, source_target_pairs={{0,4},{4,12},{12,8},{8,0},{1,5},{5,13},{13,9},{9,1},{2,6},{6,14},{... | collective-permute-start | bytes 442376 | tf_op jit(solution)/shard_map/ppermute | solution.py:316
  52.0 1.1 %copy-done.5 = bf16[4,48,1536]{2,1,0:T(8,128)(2,1)S(1)} copy-done((bf16[4,48,1536]{2,1,0:T(8,128)(2,1)S(1)}, bf16[4,48,1536]{2,1,0:T(8,128)(2,1)}, u32[]{:S(2)}) %copy-start.5) | copy-done | bytes 589848
  53.1 2.4 %mix.1 = bf16[48,4,1536]{2,1,0:T(4,128)(2,1)} custom-call(bf16[4,4,48,384]{3,2,1,0:T(8,128)(2,1)} %all-to-all-done.recv_ref, bf16[4,48,1536]{2,1,0:T(8,128)(2,1)S(1)} %copy-done.5), custom_call_target="tpu_custom_call" | custom-call | tf_op jit(solution)/shard_map/mix/pallas_call | solution.py:114
  55.5 2.3 %copy-done.1 = f32[4,192,1536]{2,1,0:T(8,128)S(1)} copy-done((f32[4,192,1536]{2,1,0:T(8,128)S(1)}, f32[4,192,1536]{2,1,0:T(8,128)}, u32[]{:S(2)}) %copy-start.1) | copy-done | bytes 4718616
  57.8 2.3 %copy-done.3 = f32[4,192,1536]{2,1,0:T(8,128)S(1)} copy-done((f32[4,192,1536]{2,1,0:T(8,128)S(1)}, f32[4,192,1536]{2,1,0:T(8,128)}, u32[]{:S(2)}) %copy-start.3) | copy-done | bytes 4718616
  60.2 0.9 copy-done.10
  61.1 0.9 copy-done.15
  62.0 8.4 %token_.4 = (bf16[4,1536,1536]{2,1,0:T(8,128)(2,1)}, bf16[192,1536]{1,0:T(8,128)(2,1)S(1)}, f32[8,1536]{1,0:T(8,128)S(1)}) custom-call(s32[4]{0:T(128)S(1)} %dynamic-slice_bitcast_fusion.idx_ref, bf16[48,1536]{1,0:T(8,128)(2,1)S(1)} %copy-done.10, bf16[48,1536]{1,0:T(8,128)(2,1)S(1)} %copy-done.15, bf16[48,1536]{1,0:T(8,128)(2,1)} %collective-permute-done.10.refs_2_, ...), custom_call_target="tpu_custom_call" | custom-call | flops 1811939328 | bytes 12976128 | tf_op jit(solution)/shard_map/token/pallas_call | solution.py:264
  70.4 8.4 %token_.5 = (bf16[4,1536,1536]{2,1,0:T(8,128)(2,1)}, bf16[192,1536]{1,0:T(8,128)(2,1)S(1)}, f32[8,1536]{1,0:T(8,128)S(1)}) custom-call(s32[4]{0:T(128)S(1)} %dynamic-slice_bitcast_fusion.idx_ref, bf16[48,1536]{1,0:T(8,128)(2,1)S(1)} %copy-done.8, bf16[48,1536]{1,0:T(8,128)(2,1)} %collective-permute-done.6.refs_1_, ...), custom_call_target="tpu_custom_call", output_to_operand_aliasing={{0}: (10, {})} | custom-call | flops 1811939328 | bytes 12976128 | tf_op jit(solution)/shard_map/token/pallas_call | solution.py:264
  78.8 8.4 %token_.6 = (bf16[4,1536,1536]{2,1,0:T(8,128)(2,1)}, bf16[192,1536]{1,0:T(8,128)(2,1)S(1)}, f32[8,1536]{1,0:T(8,128)S(1)}) custom-call(s32[4]{0:T(128)S(1)} %dynamic-slice_bitcast_fusion.idx_ref, bf16[48,1536]{1,0:T(8,128)(2,1)S(1)} %get-tuple-element.43.refs_0_, bf16[48,1536]{1,0:T(8,128)(2,1)} %collective-permute-done.3.refs_1_, ...), custom_call_target="tpu_custom_call", output_to_operand_aliasing={{0}: (10, {})} | custom-call | flops 1811939328 | bytes 12976128 | tf_op jit(solution)/shard_map/token/pallas_call | solution.py:264
  87.3 9.4 %token_.7 = (bf16[4,1536,1536]{2,1,0:T(8,128)(2,1)}, bf16[192,4,1536]{2,1,0:T(4,128)(2,1)}, f32[8,4,1536]{2,1,0:T(4,128)}) custom-call(s32[4]{0:T(128)S(1)} %dynamic-slice_bitcast_fusion.idx_ref, bf16[48,1536]{1,0:T(8,128)(2,1)S(1)} %get-tuple-element.44.refs_0_, bf16[48,1536]{1,0:T(8,128)(2,1)} %collective-permute-done.refs_1_, ...), custom_call_target="tpu_custom_call", output_to_operand_aliasing={{0}: (10, {})} | custom-call | flops 1811939328 | bytes 12976128 | tf_op jit(solution)/shard_map/token/pallas_call | solution.py:264
  (42 shorter events, 4.7 us)
Async XLA Ops:
  0.6 1.1 %copy-start.11 = (bf16[48,4,1536]{2,1,0:T(4,128)(2,1)S(1)}, bf16[48,4,1536]{2,1,0:T(4,128)(2,1)}, u32[]{:S(2)}) copy-start(bf16[48,4,1536]{2,1,0:T(4,128)(2,1)} %x_ref.1) | copy-start | bytes 1769476
  1.7 1.1 %copy-start.12 = (bf16[48,4,1536]{2,1,0:T(4,128)(2,1)S(1)}, bf16[48,4,1536]{2,1,0:T(4,128)(2,1)}, u32[]{:S(2)}) copy-start(bf16[48,4,1536]{2,1,0:T(4,128)(2,1)} %g_ref.1) | copy-start | bytes 1769476
  2.8 0.7 copy-start.16
  5.5 0.8 copy-start.4
  6.3 26.0 %copy-start.7 = (bf16[48,1536]{1,0:T(8,128)(2,1)}, bf16[48,1536]{1,0:T(8,128)(2,1)S(1)}, u32[]{:S(2)}) copy-start(bf16[48,1536]{1,0:T(8,128)(2,1)S(1)} %get-tuple-element.42.refs_0_) | copy-start | bytes 442372
  6.3 26.0 %copy-start.9 = (bf16[48,1536]{1,0:T(8,128)(2,1)}, bf16[48,1536]{1,0:T(8,128)(2,1)S(1)}, u32[]{:S(2)}) copy-start(bf16[48,1536]{1,0:T(8,128)(2,1)S(1)} %get-tuple-element.41.refs_0_) | copy-start | bytes 442372
  6.3 11.8 %collective-permute-start.9 = (bf16[48,1536]{1,0:T(8,128)(2,1)S(1)}, bf16[48,1536]{1,0:T(8,128)(2,1)S(1)}, u32[]{:S(2)}, u32[]{:S(2)}) collective-permute-start(bf16[48,1536]{1,0:T(8,128)(2,1)S(1)} %get-tuple-element.41.refs_0_), channel_id=1, source_target_pairs={{0,4},{4,12},{12,8},{8,0},{1,5},{5,13},{13,9},{9,1},{2,6},{6,14},{... | collective-permute-start | bytes 442376 | tf_op jit(solution)/shard_map/ppermute | solution.py:316
  9.3 9.6 %all-to-all-start.1 = ((f32[4,4,384]{2,1,0:T(4,128)}), f32[4,4,384]{2,1,0:T(4,128)S(1)}, u32[]{:S(2)}, u32[]{:S(2)}) async-start(f32[4,4,384]{2,1,0:T(4,128)} %get-tuple-element.40), calls=%async_computation.1 | async-start | bytes 49152 | tf_op jit(solution)/shard_map/all_to_all | solution.py:340
  13.2 10.7 %collective-permute-start.6 = (bf16[48,1536]{1,0:T(8,128)(2,1)S(1)}, bf16[48,1536]{1,0:T(8,128)(2,1)}, u32[]{:S(2)}, u32[]{:S(2)}) collective-permute-start(bf16[48,1536]{1,0:T(8,128)(2,1)S(1)} %get-tuple-element.42.refs_0_), channel_id=1, source_target_pairs={{0,4},{4,12},{12,8},{8,0},{1,5},{5,13},{13,9},{9,1},{2,6},{6,14},{... | collective-permute-start | bytes 442376 | tf_op jit(solution)/shard_map/ppermute | solution.py:316
  15.2 10.0 %collective-permute-start.3 = (bf16[48,1536]{1,0:T(8,128)(2,1)S(1)}, bf16[48,1536]{1,0:T(8,128)(2,1)}, u32[]{:S(2)}, u32[]{:S(2)}) collective-permute-start(bf16[48,1536]{1,0:T(8,128)(2,1)S(1)} %get-tuple-element.43.refs_0_), channel_id=1, source_target_pairs={{0,4},{4,12},{12,8},{8,0},{1,5},{5,13},{13,9},{9,1},{2,6},{6,14},{... | collective-permute-start | bytes 442376 | tf_op jit(solution)/shard_map/ppermute | solution.py:316
  17.6 10.3 %collective-permute-start = (bf16[48,1536]{1,0:T(8,128)(2,1)S(1)}, bf16[48,1536]{1,0:T(8,128)(2,1)}, u32[]{:S(2)}, u32[]{:S(2)}) collective-permute-start(bf16[48,1536]{1,0:T(8,128)(2,1)S(1)} %get-tuple-element.44.refs_0_), channel_id=1, source_target_pairs={{0,4},{4,12},{12,8},{8,0},{1,5},{5,13},{13,9},{9,1},{2,6},{6,14},{... | collective-permute-start | bytes 442376 | tf_op jit(solution)/shard_map/ppermute | solution.py:316
  18.2 14.1 %copy-start.14 = (bf16[48,1536]{1,0:T(8,128)(2,1)}, bf16[48,1536]{1,0:T(8,128)(2,1)S(1)}, u32[]{:S(2)}) copy-start(bf16[48,1536]{1,0:T(8,128)(2,1)S(1)} %collective-permute-done.9.refs_1_) | copy-start | bytes 442372
  18.2 12.4 %collective-permute-start.10 = (bf16[48,1536]{1,0:T(8,128)(2,1)S(1)}, bf16[48,1536]{1,0:T(8,128)(2,1)}, u32[]{:S(2)}, u32[]{:S(2)}) collective-permute-start(bf16[48,1536]{1,0:T(8,128)(2,1)S(1)} %collective-permute-done.9.refs_1_), channel_id=1, source_target_pairs={{0,4},{4,12},{12,8},{8,0},{1,5},{5,13},{13,9},{9,1},{2,6},{6,14},{... | collective-permute-start | bytes 442376 | tf_op jit(solution)/shard_map/ppermute | solution.py:316
  19.0 33.0 %all-to-all-start = ((bf16[4,4,48,384]{3,2,1,0:T(8,128)(2,1)}), bf16[4,4,48,384]{3,2,1,0:T(8,128)(2,1)}, u32[]{:S(2)}, u32[]{:S(2)}) async-start(bf16[4,4,48,384]{3,2,1,0:T(8,128)(2,1)} %get-tuple-element.23), calls=%async_computation | async-start | bytes 1179648 | tf_op jit(solution)/shard_map/all_to_all | solution.py:338
  23.9 24.1 %collective-permute-start.7 = (bf16[48,1536]{1,0:T(8,128)(2,1)}, bf16[48,1536]{1,0:T(8,128)(2,1)}, u32[]{:S(2)}, u32[]{:S(2)}) collective-permute-start(bf16[48,1536]{1,0:T(8,128)(2,1)} %collective-permute-done.6.refs_1_), channel_id=1, source_target_pairs={{0,4},{4,12},{12,8},{8,0},{1,5},{5,13},{13,9},{9,1},{2,6},{6,14},{... | collective-permute-start | bytes 442376 | tf_op jit(solution)/shard_map/ppermute | solution.py:316
  25.2 25.0 %collective-permute-start.4 = (bf16[48,1536]{1,0:T(8,128)(2,1)}, bf16[48,1536]{1,0:T(8,128)(2,1)}, u32[]{:S(2)}, u32[]{:S(2)}) collective-permute-start(bf16[48,1536]{1,0:T(8,128)(2,1)} %collective-permute-done.3.refs_1_), channel_id=1, source_target_pairs={{0,4},{4,12},{12,8},{8,0},{1,5},{5,13},{13,9},{9,1},{2,6},{6,14},{... | collective-permute-start | bytes 442376 | tf_op jit(solution)/shard_map/ppermute | solution.py:316
  27.9 22.7 %collective-permute-start.1 = (bf16[48,1536]{1,0:T(8,128)(2,1)}, bf16[48,1536]{1,0:T(8,128)(2,1)}, u32[]{:S(2)}, u32[]{:S(2)}) collective-permute-start(bf16[48,1536]{1,0:T(8,128)(2,1)} %collective-permute-done.refs_1_), channel_id=1, source_target_pairs={{0,4},{4,12},{12,8},{8,0},{1,5},{5,13},{13,9},{9,1},{2,6},{6,14},{... | collective-permute-start | bytes 442376 | tf_op jit(solution)/shard_map/ppermute | solution.py:316
  30.6 24.9 %collective-permute-start.11 = (bf16[48,1536]{1,0:T(8,128)(2,1)}, bf16[48,1536]{1,0:T(8,128)(2,1)}, u32[]{:S(2)}, u32[]{:S(2)}) collective-permute-start(bf16[48,1536]{1,0:T(8,128)(2,1)} %collective-permute-done.10.refs_2_), channel_id=1, source_target_pairs={{0,4},{4,12},{12,8},{8,0},{1,5},{5,13},{13,9},{9,1},{2,6},{6,14},{... | collective-permute-start | bytes 442376 | tf_op jit(solution)/shard_map/ppermute | solution.py:316
  32.3 1.7 %copy-start.6 = (bf16[192,4,1536]{2,1,0:T(4,128)(2,1)S(1)}, bf16[192,4,1536]{2,1,0:T(4,128)(2,1)}, u32[]{:S(2)}) copy-start(bf16[192,4,1536]{2,1,0:T(4,128)(2,1)} %pre_ref.1) | copy-start | bytes 7077892
  34.0 0.9 copy-start.13
  42.4 2.2 %copy-start = (f32[4,192,1536]{2,1,0:T(8,128)}, f32[4,192,1536]{2,1,0:T(8,128)S(1)}, u32[]{:S(2)}) copy-start(f32[4,192,1536]{2,1,0:T(8,128)S(1)} %get-tuple-element.25.refs_5_) | copy-start | bytes 14155780
  44.6 2.1 %copy-start.2 = (f32[4,192,1536]{2,1,0:T(8,128)}, f32[4,192,1536]{2,1,0:T(8,128)S(1)}, u32[]{:S(2)}) copy-start(f32[4,192,1536]{2,1,0:T(8,128)S(1)} %get-tuple-element.26.refs_6_) | copy-start | bytes 14155780
  48.1 22.3 %collective-permute-start.8 = (bf16[48,1536]{1,0:T(8,128)(2,1)}, bf16[48,1536]{1,0:T(8,128)(2,1)}, u32[]{:S(2)}, u32[]{:S(2)}) collective-permute-start(bf16[48,1536]{1,0:T(8,128)(2,1)} %collective-permute-done.7.refs_2_), channel_id=1, source_target_pairs={{0,4},{4,12},{12,8},{8,0},{1,5},{5,13},{13,9},{9,1},{2,6},{6,14},{... | collective-permute-start | bytes 442376 | tf_op jit(solution)/shard_map/ppermute | solution.py:316
  50.2 28.6 %collective-permute-start.5 = (bf16[48,1536]{1,0:T(8,128)(2,1)}, bf16[48,1536]{1,0:T(8,128)(2,1)}, u32[]{:S(2)}, u32[]{:S(2)}) collective-permute-start(bf16[48,1536]{1,0:T(8,128)(2,1)} %collective-permute-done.4.refs_2_), channel_id=1, source_target_pairs={{0,4},{4,12},{12,8},{8,0},{1,5},{5,13},{13,9},{9,1},{2,6},{6,14},{... | collective-permute-start | bytes 442376 | tf_op jit(solution)/shard_map/ppermute | solution.py:316
  50.5 36.7 %collective-permute-start.2 = (bf16[48,1536]{1,0:T(8,128)(2,1)}, bf16[48,1536]{1,0:T(8,128)(2,1)}, u32[]{:S(2)}, u32[]{:S(2)}) collective-permute-start(bf16[48,1536]{1,0:T(8,128)(2,1)} %collective-permute-done.1.refs_2_), channel_id=1, source_target_pairs={{0,4},{4,12},{12,8},{8,0},{1,5},{5,13},{13,9},{9,1},{2,6},{6,14},{... | collective-permute-start | bytes 442376 | tf_op jit(solution)/shard_map/ppermute | solution.py:316
  52.0 1.1 %copy-start.5 = (bf16[4,48,1536]{2,1,0:T(8,128)(2,1)S(1)}, bf16[4,48,1536]{2,1,0:T(8,128)(2,1)}, u32[]{:S(2)}) copy-start(bf16[4,48,1536]{2,1,0:T(8,128)(2,1)} %copy-done.4) | copy-start | bytes 1769476
  53.1 17.3 %copy-start.8 = (bf16[48,1536]{1,0:T(8,128)(2,1)S(1)}, bf16[48,1536]{1,0:T(8,128)(2,1)}, u32[]{:S(2)}) copy-start(bf16[48,1536]{1,0:T(8,128)(2,1)} %copy-done.7) | copy-start | bytes 442372
  55.5 2.3 %copy-start.1 = (f32[4,192,1536]{2,1,0:T(8,128)S(1)}, f32[4,192,1536]{2,1,0:T(8,128)}, u32[]{:S(2)}) copy-start(f32[4,192,1536]{2,1,0:T(8,128)} %copy-done) | copy-start | bytes 14155780
  57.8 2.3 %copy-start.3 = (f32[4,192,1536]{2,1,0:T(8,128)S(1)}, f32[4,192,1536]{2,1,0:T(8,128)}, u32[]{:S(2)}) copy-start(f32[4,192,1536]{2,1,0:T(8,128)} %copy-done.2) | copy-start | bytes 14155780
  60.2 0.9 copy-start.10
  61.1 0.9 copy-start.15

commit v2 on v0

v2 whole, which is shorter than its diff:
```python
import functools
import jax
import jax.numpy as jnp
from jax import lax
from jax.experimental import pallas as pl
from jax.experimental.pallas import tpu as pltpu
from jax.sharding import PartitionSpec as P

F32 = jnp.float32
BF16 = jnp.bfloat16
LIMIT = 56 << 20


def gelu_parts(value):
    square = value * value
    tangent = jnp.tanh(value * (0.7978845608 + (0.7978845608 * 0.044715) * square))
    half = 0.5 + 0.5 * tangent
    activated = value * half
    slope = half + activated * (1.0 - tangent) * (
        0.7978845608 + (0.7978845608 * 3.0 * 0.044715) * square
    )
    return activated, slope


def pin(value):
    return pltpu.with_memory_space_constraint(value, pltpu.HBM)


def ring_order(count):
    return [0] + list(range(1, count, 2)) + list(range(2, count, 2))[::-1]


def take_rows(rows_ref, t, count, toks):
    return jnp.concatenate(
        [rows_ref[j, pl.ds(t, count, stride=toks), :] for j in range(rows_ref.shape[0])], axis=1
    )


def put_rows(rows_ref, t, count, toks, value, first=0):
    for j in range(value.shape[1] // 128):
        rows_ref[first + j, pl.ds(t, count, stride=toks), :] = value[:, j * 128 : (j + 1) * 128]


def spill(rows_ref, out_ref):
    count, toks, width = out_ref.shape
    for j in range(width // 128):
        out_ref[:, :, j * 128 : (j + 1) * 128] = (
            rows_ref[j].reshape(count, toks, 128).astype(out_ref.dtype)
        )


def norm_kernel(pieces, chunks, x_hbm, g_hbm, gain_hbm, *refs):
    dz_refs, refs = refs[:chunks], refs[chunks:]
    send_refs, (gg_ref, x_ref, g_ref, gain_ref, rows_ref, sems) = refs[:-6], refs[-6:]
    count, toks, width = x_ref.shape
    gain_copy = pltpu.make_async_copy(gain_hbm, gain_ref, sems.at[2 * pieces])
    gain_copy.start()
    size = count // pieces
    copies = []
    for k in range(pieces):
        part = pl.ds(k * size, size)
        pair = (
            pltpu.make_async_copy(x_hbm.at[part], x_ref.at[part], sems.at[2 * k]),
            pltpu.make_async_copy(g_hbm.at[part], g_ref.at[part], sems.at[2 * k + 1]),
        )
        for copy in pair:
            copy.start()
        copies.append(pair)
    gain_copy.wait()
    step = 8 // toks
    gain = jnp.concatenate([gain_ref[...]] * step, axis=0)
    scale = 1.0 / width
    total = jnp.zeros((8, width), F32)
    for i in range(count // step):
        if i * step % size == 0:
            for copy in copies[i * step // size]:
                copy.wait()
        x = x_ref[i * step : (i + 1) * step].astype(F32).reshape(8, width)
        ct = g_ref[i * step : (i + 1) * step].astype(F32).reshape(8, width)
        g = ct * gain
        c = x - jnp.sum(x, axis=-1, keepdims=True) * scale
        mean_g = jnp.sum(g, axis=-1, keepdims=True) * scale
        rstd = lax.rsqrt(jnp.sum(c * c, axis=-1, keepdims=True) * scale + 1e-05)
        mean_gc = jnp.sum(g * c, axis=-1, keepdims=True) * scale
        xhat = c * rstd
        total = total + ct * xhat
        dz = rstd * (g - mean_g - xhat * (mean_gc * rstd))
        for j in range(width // 128):
            rows_ref[j, i * 8 : (i + 1) * 8, :] = dz[:, j * 128 : (j + 1) * 128]
    part = sum(total[k * toks : (k + 1) * toks] for k in range(step))
    gg_ref[...] = part
    dz = [ref.at[i] for ref in dz_refs for i in range(ref.shape[0])]
    for t in range(toks):
        dz[t][:, :width] = take_rows(rows_ref, t, count, toks).astype(BF16)
    if dz[0].shape[1] > width:
        high = part.astype(BF16).astype(F32)
        for k, value in enumerate((high, part - high)):
            lines = [
                value[i : i + 1, j : j + 128] for i in range(toks) for j in range(0, width, 128)
            ]
            dz[0][:, width + 128 * k : width + 128 * (k + 1)] = jnp.concatenate(
                lines, axis=0
            ).astype(BF16)
    me = lax.axis_index("tok")
    block = width // (1 + len(send_refs))
    for k, send_ref in enumerate(send_refs):
        start = pl.multiple_of((me ^ (k + 1)) * block, 128)
        for t in range(toks):
            send_ref[t] = dz[t][:, pl.ds(start, block)]


def norm(pre_norm, cotangent, gain, groups, chunks, spare):
    count, toks, width = pre_norm.shape
    pieces = 4
    return pl.pallas_call(
        functools.partial(norm_kernel, pieces, len(chunks)),
        out_shape=[
            jax.ShapeDtypeStruct((size, count, width + (0 if i else spare)), BF16)
            for i, size in enumerate(chunks)
        ]
        + [jax.ShapeDtypeStruct((toks, count, width // groups), BF16)] * (groups - 1)
        + [jax.ShapeDtypeStruct((toks, width), F32)],
        in_specs=[pl.BlockSpec(memory_space=pltpu.HBM)] * 3,
        out_specs=[pl.BlockSpec(memory_space=pltpu.VMEM)] * (len(chunks) + groups),
        scratch_shapes=[
            pltpu.VMEM((count, toks, width), BF16),
            pltpu.VMEM((count, toks, width), BF16),
            pltpu.VMEM((toks, width), F32),
            pltpu.VMEM((width // 128, count * toks, 128), F32),
            pltpu.SemaphoreType.DMA((2 * pieces + 1,)),
        ],
        compiler_params=pltpu.CompilerParams(vmem_limit_bytes=12 << 20),
        name="norm",
    )(pin(pre_norm), pin(cotangent), pin(gain))


def mix_kernel(groups, *refs):
    recv_refs, dz_refs, (out_ref, rows_ref) = refs[: groups - 1], refs[groups - 1 : -2], refs[-2:]
    dz_refs = [ref.at[i] for ref in dz_refs for i in range(ref.shape[0])]
    count, toks, width = out_ref.shape
    block = width // (1 + len(recv_refs))
    piece = block // toks
    me = lax.axis_index("tok")
    for k in range(1 + len(recv_refs)):
        start = pl.multiple_of((me ^ k) * block, 128)
        if k:
            got = [recv_refs[k - 1][i].astype(F32) for i in range(toks)]
        else:
            got = [dz_refs[i][:, pl.ds(start, block)].astype(F32) for i in range(toks)]
        for j in range(toks):
            mixed = jnp.concatenate(
                [got[i][:, j * piece : (j + 1) * piece] for i in range(toks)], axis=1
            )
            mixed = mixed + dz_refs[j][:, pl.ds(start, block)].astype(F32)
            put_rows(rows_ref, j, count, toks, mixed, (me ^ k) * (block // 128))
    spill(rows_ref, out_ref)


def mix(recv, dz, width):
    toks = sum(v.shape[0] for v in dz)
    count = dz[0].shape[1]
    return pl.pallas_call(
        functools.partial(mix_kernel, 1 + len(recv)),
        out_shape=jax.ShapeDtypeStruct((count, toks, width), BF16),
        in_specs=[pl.BlockSpec(memory_space=pltpu.VMEM)] * (len(recv) + len(dz)),
        out_specs=pl.BlockSpec(memory_space=pltpu.VMEM),
        scratch_shapes=[pltpu.VMEM((width // 128, count * toks, 128), F32)],
        compiler_params=pltpu.CompilerParams(vmem_limit_bytes=8 << 20),
        cost_estimate=pl.CostEstimate(flops=1, bytes_accessed=1, transcendentals=0),
        name="mix",
    )(*recv, *dz)


def one_hot(scenario_ref, count):
    return (
        lax.broadcasted_iota(jnp.int32, (count, scenario_ref.shape[1]), 0) == scenario_ref[...]
    ).astype(BF16)


def act_kernel(parts, first, toks, source, gates_hbm, pick, w_hbm, *refs):
    h_ref, act_ref, mul_ref, w_ref, refs = *refs[:4], refs[4:]
    count, width = act_ref.shape[1:]
    held = act_ref.shape[0]
    block = width // parts
    cols = block // 128
    if not first:
        hot_ref, rest_ref, pre_ref, scenario_ref, rows_ref, *refs = refs
    gates_ref, sems = refs
    copies = [pltpu.make_async_copy(gates_hbm, gates_ref, sems.at[0])]
    if not first:
        copies.append(pltpu.make_async_copy(pick, scenario_ref, sems.at[1]))
        for i in range(parts):
            part = pl.ds(i * block, block)
            copies.append(
                pltpu.make_async_copy(source.at[:, :, part], pre_ref.at[:, :, part], sems.at[2 + i])
            )
    weights = [
        pltpu.make_async_copy(w_hbm.at[first + t], w_ref.at[t], sems.at[2 + parts + t])
        for t in range(held)
    ]
    for copy in copies + weights:
        copy.start()
    copies[0].wait()
    if first:
        hot = pick[...]
    else:
        copies[1].wait()
        hot = one_hot(scenario_ref, gates_ref.shape[0])
        hot_ref[...] = hot
    hot = jnp.concatenate([hot] * 3, axis=0)
    for i in range(parts):
        part = slice(i * block, (i + 1) * block)
        if not first:
            copies[2 + i].wait()
            for j in range(cols):
                lane = i * block + j * 128
                rows_ref[j] = (
                    pre_ref[:, :, lane : lane + 128].astype(F32).reshape(count * toks, 128)
                )
            for t in range(held, toks):
                rest_ref[t - held, :, part] = take_rows(rows_ref, t, count, toks)
        for t in range(held):
            gate = gates_ref[:, first + t, part]
            high = gate.astype(BF16)
            rest = gate - high.astype(F32)
            mid = rest.astype(BF16)
            low = (rest - mid.astype(F32)).astype(BF16)
            rate = lax.dot_general(
                hot,
                jnp.concatenate([high, mid, low], axis=0),
                (((0,), (0,)), ((), ())),
                preferred_element_type=F32,
            )
            value = source[t, :, part] if first else take_rows(rows_ref, t, count, toks)
            activated, slope = gelu_parts(value)
            h_ref[t, :, part] = (activated * rate).astype(BF16)
            act_ref[t, :, part] = activated
            mul_ref[t, :, part] = rate * slope
    for copy in weights:
        copy.wait()


def activations(first, source, gates, pick, down_weight):
    scen, toks, width = gates.shape
    count = source.shape[1] if first else source.shape[0]
    held = toks // 2
    parts = width // 512
    vmem = pl.BlockSpec(memory_space=pltpu.VMEM)
    hbm = pl.BlockSpec(memory_space=pltpu.HBM)
    shapes = [
        jax.ShapeDtypeStruct((held, count, width), BF16),
        jax.ShapeDtypeStruct((held, count, width), F32),
        jax.ShapeDtypeStruct((held, count, width), F32),
        jax.ShapeDtypeStruct((held,) + down_weight.shape[1:], BF16),
    ]
    scratch = [pltpu.VMEM(gates.shape, F32), pltpu.SemaphoreType.DMA((2 + parts + held,))]
    if not first:
        shapes += [
            jax.ShapeDtypeStruct((scen, count), BF16),
            jax.ShapeDtypeStruct((toks - held, count, width), F32),
        ]
        scratch = [
            pltpu.VMEM((count, toks, width), BF16),
            pltpu.VMEM(pick.shape, jnp.int32),
            pltpu.VMEM((512 // 128, count * toks, 128), F32),
        ] + scratch
        source, pick = pin(source), pin(pick)
    return pl.pallas_call(
        functools.partial(act_kernel, parts, first, toks),
        in_specs=[vmem, hbm, vmem, hbm] if first else [hbm] * 4,
        out_specs=[vmem] * len(shapes),
        out_shape=shapes,
        scratch_shapes=scratch,
        compiler_params=pltpu.CompilerParams(vmem_limit_bytes=14 << 20),
        cost_estimate=pl.CostEstimate(flops=1, bytes_accessed=1, transcendentals=0),
        name="act",
    )(source, pin(gates), pick, pin(down_weight))


def token_kernel(t, at, parts, merge, sources, *refs):
    chunks, refs = refs[:parts], refs[parts:]
    shards = [chunk.at[at] for chunk in chunks]
    all_w, all_act, all_mul, all_h, hot_ref = refs[:5]
    w_ref, act_ref, mul_ref, h_ref = [ref.at[t % 2] for ref in (all_w, all_act, all_mul, all_h)]
    refs = refs[5:]
    if t:
        refs = refs[1:]
    done = ()
    if merge:
        done, refs = refs[: 2 * t], refs[2 * t :]
    down_hbm, pre_ref, gate_ref = refs[:3]
    refs = refs[3:]
    if not t:
        gain_ref, refs = refs[0], refs[1:]
    dz_ref, out_ref, sems = refs[:3]

    me = lax.axis_index("dp")
    size = shards[0].shape[0]
    width = dz_ref.shape[1]
    for k in range(parts):
        place = sum(jnp.where(me == m, sources[m][k], 0) for m in range(parts))
        start = pl.multiple_of(place * size, 16)
        dz_ref[pl.ds(start, size), :] = shards[k][:, :width]
    if not t:
        total = sum(shard[:, width + i : width + i + 128].astype(F32) for shard in shards for i in (0, 128))
        lines_ref = refs[3]
        lines_ref[...] = total
        share = gain_ref.shape[1] // 128
        cols = width // 128
        for i in range(gain_ref.shape[0]):
            for j in range(share):
                gain_ref[i : i + 1, j * 128 : (j + 1) * 128] = lines_ref[
                    pl.ds(i * cols + me * share + j, 1), :
                ]
    dz = dz_ref[...]
    hidden = out_ref.shape[0]
    block = hidden // 3
    hot = hot_ref[...]
    writes = []

    def write(source, target, k):
        writes.append(pltpu.make_async_copy(source, target, sems.at[k]))
        writes[-1].start()

    def down(i):
        rows = pl.ds(i * block, block)
        out_ref[i * block : (i + 1) * block] = lax.dot_general(
            h_ref[:, i * block : (i + 1) * block],
            dz,
            (((0,), (0,)), ((), ())),
            preferred_element_type=F32,
        ).astype(BF16)
        write(out_ref.at[rows], down_hbm.at[t, rows], i)

    def back(i):
        part = slice(i * block, (i + 1) * block)
        d_hidden = lax.dot_general(
            dz, w_ref[part], (((1,), (1,)), ((), ())), preferred_element_type=F32
        )
        product = d_hidden * act_ref[:, part]
        high = product.astype(BF16)
        low = (product - high.astype(F32)).astype(BF16)
        d_gate = jnp.dot(hot, high, preferred_element_type=F32) + jnp.dot(
            hot, low, preferred_element_type=F32
        )
        d_pre = d_hidden * mul_ref[:, part]
        if not merge:
            pre_ref[:, part] = d_pre.astype(BF16)
            gate_ref[:, part] = d_gate
            return
        rows_ref, spill_ref = refs[3:5]
        count, toks, _ = pre_ref.shape
        for k in range(t):
            put_rows(rows_ref, k, count, toks, done[2 * k][:, part].astype(F32))
            gate_ref[:, k, part] = done[2 * k + 1][:, part]
        put_rows(rows_ref, t, count, toks, d_pre)
        gate_ref[:, t, part] = d_gate
        if i > 1:
            writes[2 * i - 3].wait()
        spill(rows_ref, spill_ref.at[i % 2])
        write(spill_ref.at[i % 2], pre_ref.at[:, :, pl.ds(i * block, block)], 3 + i)

    for i in range(3):
        down(i)
        back(i)
    for k, copy in enumerate(writes):
        if not merge or k != 1:
            copy.wait()


def token_step(t, at, toks, sources, shards, held, act, mul, h, hot, down, done):
    hidden, width = held.shape[1:]
    scen, count = hot.shape
    parts = len(shards)
    merge = t == toks - 1
    anywhere = pl.BlockSpec(memory_space=pltpu.HBM)
    vmem = pl.BlockSpec(memory_space=pltpu.VMEM)
    operands = list(shards) + [held, act, mul, h, hot]
    specs = [vmem] * (parts + 5)
    aliases = {}
    if t:
        aliases = {len(operands): 0}
        operands.append(down)
        specs.append(anywhere)
    scratch = [
        pltpu.VMEM((count, width), BF16),
        pltpu.VMEM((hidden, width), BF16),
        pltpu.SemaphoreType.DMA((6,)),
    ]
    if merge:
        for pre, gate in done:
            operands += [pre, gate]
            specs += [vmem, vmem]
        scratch.append(pltpu.VMEM((hidden // 3 // 128, count * toks, 128), F32))
        scratch.append(pltpu.VMEM((2, count, toks, hidden // 3), BF16))
        pre_shape, gate_shape = (count, toks, hidden), (scen, toks, hidden)
    else:
        pre_shape, gate_shape = (count, hidden), (scen, hidden)
    shapes = [
        jax.ShapeDtypeStruct((toks, hidden, width), BF16),
        jax.ShapeDtypeStruct(pre_shape, BF16),
        jax.ShapeDtypeStruct(gate_shape, F32),
    ]
    if not t:
        shapes.append(jax.ShapeDtypeStruct((toks, width // parts), F32))
        scratch.append(pltpu.VMEM((shards[0].shape[1], 128), F32))
    return pl.pallas_call(
        functools.partial(token_kernel, t, at, parts, merge, sources),
        in_specs=specs,
        out_specs=[anywhere, anywhere if merge else vmem] + [vmem] * (len(shapes) - 2),
        scratch_shapes=scratch,
        out_shape=shapes,
        input_output_aliases=aliases,
        compiler_params=pltpu.CompilerParams(vmem_limit_bytes=14 << 20),
        cost_estimate=pl.CostEstimate(flops=1, bytes_accessed=1, transcendentals=0),
        name="token",
    )(*operands)


def plain_tokens(dz, pre_act, gates, down_weight, scenario):
    piece = lax.all_gather(dz, "dp", axis=1, tiled=True)
    onehot = (scenario[:, None] == jnp.arange(gates.shape[0], dtype=jnp.int32)[None, :]).astype(F32)
    rate = jnp.einsum("bs,stf->btf", onehot, gates, precision=lax.Precision.HIGHEST)
    activated, slope = gelu_parts(pre_act.astype(F32))
    hidden = (activated * rate).astype(BF16)
    d_hidden = jnp.einsum("tbc,tfc->btf", piece, down_weight, preferred_element_type=F32)
    gate = jnp.einsum("bs,btf->stf", onehot, d_hidden * activated, precision=lax.Precision.HIGHEST)
    pre = (d_hidden * rate * slope).astype(BF16)
    down = jnp.einsum("btf,tbc->tfc", hidden, piece, preferred_element_type=F32).astype(BF16)
    return pre, down, gate


def after(value, *others):
    return lax.optimization_barrier((value, *others))[0]


def swap(send):
    groups = 1 + len(send)
    return [
        lax.ppermute(v, "tok", [(p, p ^ (k + 1)) for p in range(groups)]) for k, v in enumerate(send)
    ]


def ring_tokens(dz, send, pre_act, gates, down_weight, scenario):
    dp = lax.axis_size("dp")
    order = ring_order(dp)
    ring = [(order[k], order[(k + 1) % dp]) for k in range(dp)]
    place = {device: k for k, device in enumerate(order)}
    sources = [[order[(place[m] - s) % dp] for s in range(dp)] for m in range(dp)]
    shards = [[v] for v in dz]

    def hop(i, *others):
        last = shards[i][-1]
        shards[i].append(lax.ppermute(after(last, *others) if others else last, "dp", ring))

    for i in range(4):
        hop(i)
    recv = swap(send)
    h, act, mul, held, hot, rest = [
        [v] for v in activations(0, pre_act, gates, scenario.reshape(1, -1), down_weight)
    ]
    hop(0, h[0])
    hop(1, h[0])
    hot, rest = hot[0], rest[0]
    more = activations(2, rest, gates, hot, down_weight)
    for have, new in zip((h, act, mul, held), more):
        have.append(new)
    d_input = mix([after(r, h[0]) for r in recv], dz, down_weight.shape[2])
    hop(2)
    hop(3)
    hop(0)
    hop(1, h[1])
    hot = after(hot, d_input)

    down, done = None, []
    homes = [(i, k) for i, v in enumerate(dz) for k in range(v.shape[0])]
    for t, (i, at) in enumerate(homes):
        down, pre, gate, *more = token_step(
            t, at, len(homes), sources, shards[i], held[t // 2], act[t // 2], mul[t // 2], h[t // 2], hot, down, done
        )
        done.append((pre, gate))
        if t == 0:
            gain_gradient = more[0]
            hop(2, gate)
        if t == 1:
            hop(3, gate)
    return d_input, pre, down, gate, gain_gradient


def per_device(pre_norm, cotangent, gain, pre_act, gates, down_weight, scenario):
    groups = lax.axis_size("tok")
    toks, width = gain.shape
    fits = down_weight.shape[1] == 1536 and toks == 4 and lax.axis_size("dp") == 4
    chunks, spare = ((1, 1, 1, 1), 256) if fits else ((toks,), 0)
    outs = norm(pre_norm, cotangent, gain, groups, chunks, spare)
    dz, send, gain_part = outs[: len(chunks)], outs[len(chunks) : -1], outs[-1]
    if fits:
        return ring_tokens(dz, send, pre_act, gates, down_weight, scenario)
    d_input = mix(swap(send), dz, width)
    pre, down, gate = plain_tokens(dz[0], pre_act, gates, down_weight, scenario)
    gain_gradient = lax.psum_scatter(gain_part, "dp", scatter_dimension=1, tiled=True)
    return d_input, pre, down, gate, gain_gradient


def solution(mesh):
    placed = (
        P(("group", "dp"), "tok", None),
        P(("group", "dp"), "tok", None),
        P("tok", None),
        P("group", "tok", "dp"),
        P(None, "tok", "dp"),
        P("tok", "dp", None),
        P("group"),
    )
    return jax.shard_map(
        per_device,
        mesh=mesh,
        in_specs=placed,
        out_specs=(
            P(("group", "dp"), "tok", None),
            P("group", "tok", "dp"),
            P(("group", "tok"), "dp", None),
            P("group", "tok", "dp"),
            P(("group", "tok"), "dp"),
        ),
        check_vma=False,
    )
```

time: 136 us -> 58 us (0.43)
  waiting for transfers between devices: 55 us -> 7.05 us
  matrix products: 33.8 us -> 0 us
  Pallas kernels: 0 us -> 31.6 us
  local copies, waits for them, and re-layouts: 21.3 us -> 0 us
  starting transfers between devices: 4.29 us -> 18.3 us
  between operations: 14.1 us -> 0.9 us
  other arithmetic: 7.26 us -> 0 us
    all_gather x1 -> x0, waiting for transfers between devices: 41.6 us -> none  [per_device(): lax.all_gather(dz_b, 'dp', axis=0, tiled=True)]
    dot_general x4 -> x0, matrix products: 33.8 us -> none  [the longest x1 12.8 us: folder(): jnp.einsum('btf,btc->tfc', hidden, piece, preferred_element_type=jnp.floa...]
    pallas_call x0 -> x8, Pallas kernels: none -> 31.6 us  [the longest x4 18.8 us: token_step(): pl.pallas_call(functools.partial(token_kernel, t, at, parts, merge, sourc...]
    ppermute x0 -> x15, starting transfers between devices: none -> 18.3 us  [the longest x12 16.4 us: hop(): lax.ppermute(after(last, *others) if others else last, 'dp', ring)]
    unnamed x3 -> x0, waiting for transfers between devices: 13.4 us -> none
    unnamed x19 -> x0, local copies, waits for them, and re-layouts: 13.1 us -> none
    convert_element_type x5 -> x0, local copies, waits for them, and re-layouts: 8.26 us -> none  [the longest x4 5.74 us: per_device(): mixed.astype(jnp.float32)]
    ppermute x0 -> x15, waiting for transfers between devices: none -> 7.05 us  [the longest x12 7.04 us: hop(): lax.ppermute(after(last, *others) if others else last, 'dp', ring)]
  transfers between devices with their start and end apart: 3 -> 15, of which waited for: 2 -> 6; matrix products, arithmetic and copies ran while one was open for 14% -> 0% of each run, Pallas kernels for 0% -> 39%
where the time goes in v2:
time: 58 us; the launch traced here: 57.9 us
  Pallas kernels  31.6 us (54%)
  starting transfers between devices  18.3 us (32%)
  waiting for transfers between devices  7.05 us (12%)
  between operations  0.9 us (2%)
    pallas_call x4, Pallas kernels, token_step(): pl.pallas_call(functools.partial(token_kernel, t, at, parts, merge, sourc...  18.8 us
    ppermute x12, starting transfers between devices, hop(): lax.ppermute(after(last, *others) if others else last, 'dp', ring)  16.4 us
    pallas_call x2, Pallas kernels, activations(): pl.pallas_call(functools.partial(act_kernel, parts, first, toks), in_spec...  8.55 us
    ppermute x12, waiting for transfers between devices, hop(): lax.ppermute(after(last, *others) if others else last, 'dp', ring)  7.04 us
    pallas_call x1, Pallas kernels, norm(): pl.pallas_call(functools.partial(norm_kernel, pieces, len(chunks)), out_s...  2.98 us
    ppermute x3, starting transfers between devices, swap(): lax.ppermute(v, 'tok', [(p, p ^ k + 1) for p in range(groups)])  1.93 us
    pallas_call x1, Pallas kernels, mix(): pl.pallas_call(functools.partial(mix_kernel, 1 + len(recv)), out_shape=ja...  1.33 us
  transfers between devices with their start and end apart: 15, of which 6 were waited for; matrix products, arithmetic and copies ran while one was open for 0% of the time, Pallas kernels for 39%

profile of v2, /device:TPU:0, one launch (start us, length us, event | category | flops | bytes accessed | tf_op | source)
XLA Modules:
  0.0 57.9 jit_solution(6351836614577820644)
XLA Ops:
  0.6 3.0 %norm.1 = (bf16[1,48,1792]{2,1,0:T(8,128)(2,1)S(1)}, bf16[1,48,1536]{2,1,0:T(8,128)(2,1)S(1)}, bf16[1,48,1536]{2,1,0:T(8,128)(2,1)S(1)}, bf16[1,48,1536]{2,1,0:T...) custom-call(bf16[48,4,1536]{2,1,0:T(4,128)(2,1)} %x_hbm.1, ...), custom_call_target="tpu_custom_call" | custom-call | tf_op jit(solution)/shard_map/norm/pallas_call | solution.py:115
  3.6 3.1 %collective-permute-start.8 = (bf16[1,48,1792]{2,1,0:T(8,128)(2,1)S(1)}, bf16[1,48,1792]{2,1,0:T(8,128)(2,1)S(1)}, u32[]{:S(2)}, u32[]{:S(2)}) collective-permute-start(bf16[1,48,1792]{2,1,0:T(8,128)(2,1)S(1)} %get-tuple-element.51.refs_3_.refs_0_), channel_id=1, source_target_pairs={{0,4},{4,12},{12,8},{8,0},{1,5},{5,13},{13,9},{9,1},{2,6},{6,14},{... | collective-permute-start | bytes 516104 | tf_op jit(solution)/shard_map/ppermute | solution.py:454
  6.7 2.6 %collective-permute-start.5 = (bf16[1,48,1536]{2,1,0:T(8,128)(2,1)S(1)}, bf16[1,48,1536]{2,1,0:T(8,128)(2,1)S(1)}, u32[]{:S(2)}, u32[]{:S(2)}) collective-permute-start(bf16[1,48,1536]{2,1,0:T(8,128)(2,1)S(1)} %get-tuple-element.52.refs_4_.refs_0_), channel_id=1, source_target_pairs={{0,4},{4,12},{12,8},{8,0},{1,5},{5,13},{13,9},{9,1},{2,6},{6,14},{... | collective-permute-start | bytes 442376 | tf_op jit(solution)/shard_map/ppermute | solution.py:454
  9.3 0.0 collective-permute-start
  9.3 4.6 %act.2 = (bf16[2,192,1536]{2,1,0:T(8,128)(2,1)S(1)}, f32[2,192,1536]{2,1,0:T(8,128)S(1)}, f32[2,192,1536]{2,1,0:T(8,128)S(1)}, bf16[2,1536,1536]{2,1,0:T(8,128)(...) custom-call(bf16[192,4,1536]{2,1,0:T(4,128)(2,1)} %source.1, f32[8,4,1536]{2,1,0:T(4,128)} %gates_hbm.3, ...), custom_call_target="tpu_custom_call" | custom-call | flops 1 | bytes 1 | tf_op jit(solution)/shard_map/act/pallas_call | solution.py:268
  13.9 0.5 collective-permute-start.9
  14.4 3.0 %collective-permute-start.12 = (bf16[1,48,1536]{2,1,0:T(8,128)(2,1)S(1)}, bf16[1,48,1536]{2,1,0:T(8,128)(2,1)S(1)}, u32[]{:S(2)}, u32[]{:S(2)}) collective-permute-start(bf16[1,48,1536]{2,1,0:T(8,128)(2,1)S(1)} %get-tuple-element.53.refs_5_.refs_0_), channel_id=1, source_target_pairs={{0,4},{4,12},{12,8},{8,0},{1,5},{5,13},{13,9},{9,1},{2,6},{6,14},{... | collective-permute-start | bytes 442376 | tf_op jit(solution)/shard_map/ppermute | solution.py:454
  17.5 0.0 collective-permute-start.6
  17.5 1.5 %collective-permute-start.1 = (bf16[4,48,384]{2,1,0:T(8,128)(2,1)S(1)}, bf16[4,48,384]{2,1,0:T(8,128)(2,1)S(1)}, u32[]{:S(2)}, u32[]{:S(2)}) collective-permute-start(bf16[4,48,384]{2,1,0:T(8,128)(2,1)S(1)} %get-tuple-element.47), channel_id=1, source_target_pairs={{0,2},{1,3},{2,0},{3,1},{4,6},{5,7},{6,4},{7,5},{8,10},{9,11},{10,... | collective-permute-start | bytes 442376 | tf_op jit(solution)/shard_map/ppermute | solution.py:440
  19.0 2.6 %collective-permute-start.3 = (bf16[1,48,1536]{2,1,0:T(8,128)(2,1)S(1)}, bf16[1,48,1536]{2,1,0:T(8,128)(2,1)S(1)}, u32[]{:S(2)}, u32[]{:S(2)}) collective-permute-start(bf16[1,48,1536]{2,1,0:T(8,128)(2,1)S(1)} %get-tuple-element.54.refs_6_.refs_0_), channel_id=1, source_target_pairs={{0,4},{4,12},{12,8},{8,0},{1,5},{5,13},{13,9},{9,1},{2,6},{6,14},{... | collective-permute-start | bytes 442376 | tf_op jit(solution)/shard_map/ppermute | solution.py:454
  21.6 0.5 collective-permute-done.9.refs_2_
  22.1 0.2 collective-permute-start.10
  22.3 2.9 %collective-permute-done.12.refs_1_ = bf16[1,48,1536]{2,1,0:T(8,128)(2,1)S(1)} collective-permute-done((bf16[1,48,1536]{2,1,0:T(8,128)(2,1)S(1)}, bf16[1,48,1536]{2,1,0:T(8,128)(2,1)S(1)}, u32[]{:S(2)}, u32[]{:S(2)}) %collective-permute-start.12) | collective-permute-done | bytes 147488 | tf_op jit(solution)/shard_map/ppermute | solution.py:454
  25.2 0.4 collective-permute-start.2
  25.7 3.9 %act.3 = (bf16[2,192,1536]{2,1,0:T(8,128)(2,1)S(1)}, f32[2,192,1536]{2,1,0:T(8,128)S(1)}, f32[2,192,1536]{2,1,0:T(8,128)S(1)}, bf16[2,1536,1536]{2,1,0:T(8,128)(2,1)S(1)}) custom-call(f32[2,192,1536]{2,1,0:T(8,128)S(1)} %get-tuple-element.56.source, f32[8,4,1536]{2,1,0:T(4,128)} %gates_hbm.3, bf16[8,192]{1,0:T(8,128)(2,1)S(1)} %get-tuple-element.63.pick.refs_8_, ...), custom_call_target="tpu_custom_call" | custom-call | flops 1 | bytes 1 | tf_op jit(solution)/shard_map/act/pallas_call | solution.py:268
  29.6 0.0 collective-permute-done.6.refs_2_
  29.6 0.1 collective-permute-start.13
  29.7 0.0 collective-permute-done.1.refs_1_
  29.7 3.2 %collective-permute-start.7 = (bf16[1,48,1536]{2,1,0:T(8,128)(2,1)S(1)}, bf16[1,48,1536]{2,1,0:T(8,128)(2,1)S(1)}, u32[]{:S(2)}, u32[]{:S(2)}) collective-permute-start(bf16[1,48,1536]{2,1,0:T(8,128)(2,1)S(1)} %collective-permute-done.6.refs_2_), channel_id=1, source_target_pairs={{0,4},{4,12},{12,8},{8,0},{1,5},{5,13},{13,9},{9,1},{2,6},{6,14},{... | collective-permute-start | bytes 442376 | tf_op jit(solution)/shard_map/ppermute | solution.py:454
  32.8 0.0 collective-permute-done.3.refs_1_
  32.8 0.1 collective-permute-start.4
  32.9 1.3 %mix.1 = bf16[48,4,1536]{2,1,0:T(4,128)(2,1)} custom-call(bf16[4,48,384]{2,1,0:T(8,128)(2,1)S(1)} %collective-permute-done.refs_0_, bf16[4,48,384]{2,1,0:T(8,128)(2,1)S(1)} %collective-permute-done.1.refs_1_, bf16[4,48,384]{2,1,0:T(8,128)(2,1)S(1)} %collective-permute-done.2.refs_2_, bf16[1,48,1792]{2,1,0:T(8,128)(2,1)S(1)} %get-tuple-element.51.refs_3_.refs_0_, ...), custom_call_target="tpu_custom_call" | custom-call | flops 1 | bytes 1 | tf_op jit(solution)/shard_map/mix/pallas_call | solution.py:162
  34.2 1.0 %collective-permute-done.10.refs_3_ = bf16[1,48,1792]{2,1,0:T(8,128)(2,1)S(1)} collective-permute-done((bf16[1,48,1792]{2,1,0:T(8,128)(2,1)S(1)}, bf16[1,48,1792]{2,1,0:T(8,128)(2,1)S(1)}, u32[]{:S(2)}, u32[]{:S(2)}) %collective-permute-start.10) | collective-permute-done | bytes 172064 | tf_op jit(solution)/shard_map/ppermute | solution.py:454
  35.2 4.7 %token_.4 = (bf16[4,1536,1536]{2,1,0:T(8,128)(2,1)}, bf16[192,1536]{1,0:T(8,128)(2,1)S(1)}, f32[8,1536]{1,0:T(8,128)S(1)}, f32[4,384]{1,0:T(4,128)}) custom-call(bf16[1,48,1792]{2,1,0:T(8,128)(2,1)S(1)} %get-tuple-element.51.refs_3_.refs_0_, bf16[1,48,1792]{2,1,0:T(8,128)(2,1)S(1)} %collective-permute-done.8.refs_1_, ...), custom_call_target="tpu_custom_call" | custom-call | flops 1 | bytes 1 | tf_op jit(solution)/shard_map/token/pallas_call | solution.py:407
  39.9 1.0 %collective-permute-start.14 = (bf16[1,48,1536]{2,1,0:T(8,128)(2,1)S(1)}, bf16[1,48,1536]{2,1,0:T(8,128)(2,1)S(1)}, u32[]{:S(2)}, u32[]{:S(2)}) collective-permute-start(bf16[1,48,1536]{2,1,0:T(8,128)(2,1)S(1)} %collective-permute-done.13.refs_2_), channel_id=1, source_target_pairs={{0,4},{4,12},{12,8},{8,0},{1,5},{5,13},{13,9},{9,1},{2,6},{6,14},{... | collective-permute-start | bytes 442376 | tf_op jit(solution)/shard_map/ppermute | solution.py:454
  40.9 0.7 %collective-permute-done.7.refs_3_ = bf16[1,48,1536]{2,1,0:T(8,128)(2,1)S(1)} collective-permute-done((bf16[1,48,1536]{2,1,0:T(8,128)(2,1)S(1)}, bf16[1,48,1536]{2,1,0:T(8,128)(2,1)S(1)}, u32[]{:S(2)}, u32[]{:S(2)}) %collective-permute-start.7) | collective-permute-done | bytes 147488 | tf_op jit(solution)/shard_map/ppermute | solution.py:454
  41.5 4.0 %token_.5 = (bf16[4,1536,1536]{2,1,0:T(8,128)(2,1)}, bf16[192,1536]{1,0:T(8,128)(2,1)S(1)}, f32[8,1536]{1,0:T(8,128)S(1)}) custom-call(bf16[1,48,1536]{2,1,0:T(8,128)(2,1)S(1)} %get-tuple-element.52.refs_4_.refs_0_, bf16[1,48,1536]{2,1,0:T(8,128)(2,1)S(1)} %collective-permute-done.5.refs_1_, ...), custom_call_target="tpu_custom_call", output_to_operand_aliasing={{0}: (9, {})} | custom-call | flops 1 | bytes 1 | tf_op jit(solution)/shard_map/token/pallas_call | solution.py:407
  45.6 0.1 collective-permute-start.11
  45.7 1.8 %collective-permute-done.14.refs_3_ = bf16[1,48,1536]{2,1,0:T(8,128)(2,1)S(1)} collective-permute-done((bf16[1,48,1536]{2,1,0:T(8,128)(2,1)S(1)}, bf16[1,48,1536]{2,1,0:T(8,128)(2,1)S(1)}, u32[]{:S(2)}, u32[]{:S(2)}) %collective-permute-start.14) | collective-permute-done | bytes 147488 | tf_op jit(solution)/shard_map/ppermute | solution.py:454
  47.5 4.0 %token_.6 = (bf16[4,1536,1536]{2,1,0:T(8,128)(2,1)}, bf16[192,1536]{1,0:T(8,128)(2,1)S(1)}, f32[8,1536]{1,0:T(8,128)S(1)}) custom-call(bf16[1,48,1536]{2,1,0:T(8,128)(2,1)S(1)} %get-tuple-element.53.refs_5_.refs_0_, bf16[1,48,1536]{2,1,0:T(8,128)(2,1)S(1)} %collective-permute-done.12.refs_1_, ...), custom_call_target="tpu_custom_call", output_to_operand_aliasing={{0}: (9, {})} | custom-call | flops 1 | bytes 1 | tf_op jit(solution)/shard_map/token/pallas_call | solution.py:407
  51.5 0.2 collective-permute-done.11.refs_3_
  51.7 6.0 %token_.7 = (bf16[4,1536,1536]{2,1,0:T(8,128)(2,1)}, bf16[192,4,1536]{2,1,0:T(4,128)(2,1)}, f32[8,4,1536]{2,1,0:T(4,128)}) custom-call(bf16[1,48,1536]{2,1,0:T(8,128)(2,1)S(1)} %get-tuple-element.54.refs_6_.refs_0_, bf16[1,48,1536]{2,1,0:T(8,128)(2,1)S(1)} %collective-permute-done.3.refs_1_, ...), custom_call_target="tpu_custom_call", output_to_operand_aliasing={{0}: (9, {})} | custom-call | flops 1 | bytes 1 | tf_op jit(solution)/shard_map/token/pallas_call | solution.py:407
  (6 shorter events, 0.0 us)
Async XLA Ops:
  3.6 10.3 %collective-permute-start.8 = (bf16[1,48,1792]{2,1,0:T(8,128)(2,1)S(1)}, bf16[1,48,1792]{2,1,0:T(8,128)(2,1)S(1)}, u32[]{:S(2)}, u32[]{:S(2)}) collective-permute-start(bf16[1,48,1792]{2,1,0:T(8,128)(2,1)S(1)} %get-tuple-element.51.refs_3_.refs_0_), channel_id=1, source_target_pairs={{0,4},{4,12},{12,8},{8,0},{1,5},{5,13},{13,9},{9,1},{2,6},{6,14},{... | collective-permute-start | bytes 516104 | tf_op jit(solution)/shard_map/ppermute | solution.py:454
  6.7 10.8 %collective-permute-start.5 = (bf16[1,48,1536]{2,1,0:T(8,128)(2,1)S(1)}, bf16[1,48,1536]{2,1,0:T(8,128)(2,1)S(1)}, u32[]{:S(2)}, u32[]{:S(2)}) collective-permute-start(bf16[1,48,1536]{2,1,0:T(8,128)(2,1)S(1)} %get-tuple-element.52.refs_4_.refs_0_), channel_id=1, source_target_pairs={{0,4},{4,12},{12,8},{8,0},{1,5},{5,13},{13,9},{9,1},{2,6},{6,14},{... | collective-permute-start | bytes 442376 | tf_op jit(solution)/shard_map/ppermute | solution.py:454
  9.3 9.7 %collective-permute-start = (bf16[4,48,384]{2,1,0:T(8,128)(2,1)S(1)}, bf16[4,48,384]{2,1,0:T(8,128)(2,1)S(1)}, u32[]{:S(2)}, u32[]{:S(2)}) collective-permute-start(bf16[4,48,384]{2,1,0:T(8,128)(2,1)S(1)} %get-tuple-element.44), channel_id=1, source_target_pairs={{0,1},{1,0},{2,3},{3,2},{4,5},{5,4},{6,7},{7,6},{8,9},{9,8},{10,11... | collective-permute-start | bytes 442376 | tf_op jit(solution)/shard_map/ppermute | solution.py:440
  13.9 8.1 %collective-permute-start.9 = (bf16[1,48,1792]{2,1,0:T(8,128)(2,1)S(1)}, bf16[1,48,1792]{2,1,0:T(8,128)(2,1)S(1)}, u32[]{:S(2)}, u32[]{:S(2)}) collective-permute-start(bf16[1,48,1792]{2,1,0:T(8,128)(2,1)S(1)} %collective-permute-done.8.refs_1_), channel_id=1, source_target_pairs={{0,4},{4,12},{12,8},{8,0},{1,5},{5,13},{13,9},{9,1},{2,6},{6,14},{... | collective-permute-start | bytes 516104 | tf_op jit(solution)/shard_map/ppermute | solution.py:454
  14.4 10.8 %collective-permute-start.12 = (bf16[1,48,1536]{2,1,0:T(8,128)(2,1)S(1)}, bf16[1,48,1536]{2,1,0:T(8,128)(2,1)S(1)}, u32[]{:S(2)}, u32[]{:S(2)}) collective-permute-start(bf16[1,48,1536]{2,1,0:T(8,128)(2,1)S(1)} %get-tuple-element.53.refs_5_.refs_0_), channel_id=1, source_target_pairs={{0,4},{4,12},{12,8},{8,0},{1,5},{5,13},{13,9},{9,1},{2,6},{6,14},{... | collective-permute-start | bytes 442376 | tf_op jit(solution)/shard_map/ppermute | solution.py:454
  17.5 12.1 %collective-permute-start.6 = (bf16[1,48,1536]{2,1,0:T(8,128)(2,1)S(1)}, bf16[1,48,1536]{2,1,0:T(8,128)(2,1)S(1)}, u32[]{:S(2)}, u32[]{:S(2)}) collective-permute-start(bf16[1,48,1536]{2,1,0:T(8,128)(2,1)S(1)} %collective-permute-done.5.refs_1_), channel_id=1, source_target_pairs={{0,4},{4,12},{12,8},{8,0},{1,5},{5,13},{13,9},{9,1},{2,6},{6,14},{... | collective-permute-start | bytes 442376 | tf_op jit(solution)/shard_map/ppermute | solution.py:454
  17.5 12.2 %collective-permute-start.1 = (bf16[4,48,384]{2,1,0:T(8,128)(2,1)S(1)}, bf16[4,48,384]{2,1,0:T(8,128)(2,1)S(1)}, u32[]{:S(2)}, u32[]{:S(2)}) collective-permute-start(bf16[4,48,384]{2,1,0:T(8,128)(2,1)S(1)} %get-tuple-element.47), channel_id=1, source_target_pairs={{0,2},{1,3},{2,0},{3,1},{4,6},{5,7},{6,4},{7,5},{8,10},{9,11},{10,... | collective-permute-start | bytes 442376 | tf_op jit(solution)/shard_map/ppermute | solution.py:440
  19.0 13.8 %collective-permute-start.3 = (bf16[1,48,1536]{2,1,0:T(8,128)(2,1)S(1)}, bf16[1,48,1536]{2,1,0:T(8,128)(2,1)S(1)}, u32[]{:S(2)}, u32[]{:S(2)}) collective-permute-start(bf16[1,48,1536]{2,1,0:T(8,128)(2,1)S(1)} %get-tuple-element.54.refs_6_.refs_0_), channel_id=1, source_target_pairs={{0,4},{4,12},{12,8},{8,0},{1,5},{5,13},{13,9},{9,1},{2,6},{6,14},{... | collective-permute-start | bytes 442376 | tf_op jit(solution)/shard_map/ppermute | solution.py:454
  22.1 13.2 %collective-permute-start.10 = (bf16[1,48,1792]{2,1,0:T(8,128)(2,1)S(1)}, bf16[1,48,1792]{2,1,0:T(8,128)(2,1)S(1)}, u32[]{:S(2)}, u32[]{:S(2)}) collective-permute-start(bf16[1,48,1792]{2,1,0:T(8,128)(2,1)S(1)} %collective-permute-done.9.refs_2_), channel_id=1, source_target_pairs={{0,4},{4,12},{12,8},{8,0},{1,5},{5,13},{13,9},{9,1},{2,6},{6,14},{... | collective-permute-start | bytes 516104 | tf_op jit(solution)/shard_map/ppermute | solution.py:454
  25.2 7.7 %collective-permute-start.2 = (bf16[4,48,384]{2,1,0:T(8,128)(2,1)S(1)}, bf16[4,48,384]{2,1,0:T(8,128)(2,1)S(1)}, u32[]{:S(2)}, u32[]{:S(2)}) collective-permute-start(bf16[4,48,384]{2,1,0:T(8,128)(2,1)S(1)} %get-tuple-element.49), channel_id=1, source_target_pairs={{0,3},{1,2},{2,1},{3,0},{4,7},{5,6},{6,5},{7,4},{8,11},{9,10},{10,... | collective-permute-start | bytes 442376 | tf_op jit(solution)/shard_map/ppermute | solution.py:440
  29.6 10.3 %collective-permute-start.13 = (bf16[1,48,1536]{2,1,0:T(8,128)(2,1)S(1)}, bf16[1,48,1536]{2,1,0:T(8,128)(2,1)S(1)}, u32[]{:S(2)}, u32[]{:S(2)}) collective-permute-start(bf16[1,48,1536]{2,1,0:T(8,128)(2,1)S(1)} %collective-permute-done.12.refs_1_), channel_id=1, source_target_pairs={{0,4},{4,12},{12,8},{8,0},{1,5},{5,13},{13,9},{9,1},{2,6},{6,14},{... | collective-permute-start | bytes 442376 | tf_op jit(solution)/shard_map/ppermute | solution.py:454
  29.7 11.9 %collective-permute-start.7 = (bf16[1,48,1536]{2,1,0:T(8,128)(2,1)S(1)}, bf16[1,48,1536]{2,1,0:T(8,128)(2,1)S(1)}, u32[]{:S(2)}, u32[]{:S(2)}) collective-permute-start(bf16[1,48,1536]{2,1,0:T(8,128)(2,1)S(1)} %collective-permute-done.6.refs_2_), channel_id=1, source_target_pairs={{0,4},{4,12},{12,8},{8,0},{1,5},{5,13},{13,9},{9,1},{2,6},{6,14},{... | collective-permute-start | bytes 442376 | tf_op jit(solution)/shard_map/ppermute | solution.py:454
  32.8 12.8 %collective-permute-start.4 = (bf16[1,48,1536]{2,1,0:T(8,128)(2,1)S(1)}, bf16[1,48,1536]{2,1,0:T(8,128)(2,1)S(1)}, u32[]{:S(2)}, u32[]{:S(2)}) collective-permute-start(bf16[1,48,1536]{2,1,0:T(8,128)(2,1)S(1)} %collective-permute-done.3.refs_1_), channel_id=1, source_target_pairs={{0,4},{4,12},{12,8},{8,0},{1,5},{5,13},{13,9},{9,1},{2,6},{6,14},{... | collective-permute-start | bytes 442376 | tf_op jit(solution)/shard_map/ppermute | solution.py:454
  39.9 7.6 %collective-permute-start.14 = (bf16[1,48,1536]{2,1,0:T(8,128)(2,1)S(1)}, bf16[1,48,1536]{2,1,0:T(8,128)(2,1)S(1)}, u32[]{:S(2)}, u32[]{:S(2)}) collective-permute-start(bf16[1,48,1536]{2,1,0:T(8,128)(2,1)S(1)} %collective-permute-done.13.refs_2_), channel_id=1, source_target_pairs={{0,4},{4,12},{12,8},{8,0},{1,5},{5,13},{13,9},{9,1},{2,6},{6,14},{... | collective-permute-start | bytes 442376 | tf_op jit(solution)/shard_map/ppermute | solution.py:454
  45.6 6.1 %collective-permute-start.11 = (bf16[1,48,1536]{2,1,0:T(8,128)(2,1)S(1)}, bf16[1,48,1536]{2,1,0:T(8,128)(2,1)S(1)}, u32[]{:S(2)}, u32[]{:S(2)}) collective-permute-start(bf16[1,48,1536]{2,1,0:T(8,128)(2,1)S(1)} %collective-permute-done.4.refs_2_), channel_id=1, source_target_pairs={{0,4},{4,12},{12,8},{8,0},{1,5},{5,13},{13,9},{9,1},{2,6},{6,14},{... | collective-permute-start | bytes 442376 | tf_op jit(solution)/shard_map/ppermute | solution.py:454

commit v3 on v2

--- a/solution.py
+++ b/solution.py
@@ -284,12 +284,14 @@
     w_ref, act_ref, mul_ref, h_ref = [ref.at[t % 2] for ref in (all_w, all_act, all_mul, all_h)]
     refs = refs[5:]
     if t:
-        refs = refs[1:]
+        refs = refs[2:]
     done = ()
     if merge:
-        done, refs = refs[: 2 * t], refs[2 * t :]
-    down_hbm, pre_ref, gate_ref = refs[:3]
+        done, refs = refs[:t], refs[t:]
+    down_hbm, rows_ref, gate_ref = refs[:3]
     refs = refs[3:]
+    if merge:
+        pre_ref, refs = refs[0], refs[1:]
     if not t:
         gain_ref, refs = refs[0], refs[1:]
     dz_ref, out_ref, sems = refs[:3]
@@ -344,20 +346,20 @@
             hot, low, preferred_element_type=F32
         )
         d_pre = d_hidden * mul_ref[:, part]
+        count = d_pre.shape[0]
+        toks = rows_ref.shape[1] // count
+        cols = block // 128
+        put_rows(rows_ref, t, count, toks, d_pre, i * cols)
         if not merge:
-            pre_ref[:, part] = d_pre.astype(BF16)
             gate_ref[:, part] = d_gate
             return
-        rows_ref, spill_ref = refs[3:5]
-        count, toks, _ = pre_ref.shape
+        spill_ref = refs[3]
         for k in range(t):
-            put_rows(rows_ref, k, count, toks, done[2 * k][:, part].astype(F32))
-            gate_ref[:, k, part] = done[2 * k + 1][:, part]
-        put_rows(rows_ref, t, count, toks, d_pre)
+            gate_ref[:, k, part] = done[k][:, part]
         gate_ref[:, t, part] = d_gate
         if i > 1:
             writes[2 * i - 3].wait()
-        spill(rows_ref, spill_ref.at[i % 2])
+        spill(rows_ref.at[i * cols : (i + 1) * cols], spill_ref.at[i % 2])
         write(spill_ref.at[i % 2], pre_ref.at[:, :, pl.ds(i * block, block)], 3 + i)
 
     for i in range(3):
@@ -379,35 +381,38 @@
     specs = [vmem] * (parts + 5)
     aliases = {}
     if t:
-        aliases = {len(operands): 0}
-        operands.append(down)
-        specs.append(anywhere)
+        aliases = {len(operands): 0, len(operands) + 1: 1}
+        operands += list(down)
+        specs += [anywhere, vmem]
     scratch = [
         pltpu.VMEM((count, width), BF16),
         pltpu.VMEM((hidden, width), BF16),
         pltpu.SemaphoreType.DMA((6,)),
     ]
     if merge:
-        for pre, gate in done:
-            operands += [pre, gate]
-            specs += [vmem, vmem]
-        scratch.append(pltpu.VMEM((hidden // 3 // 128, count * toks, 128), F32))
+        operands += list(done)
+        specs += [vmem] * t
         scratch.append(pltpu.VMEM((2, count, toks, hidden // 3), BF16))
-        pre_shape, gate_shape = (count, toks, hidden), (scen, toks, hidden)
+        gate_shape = (scen, toks, hidden)
     else:
-        pre_shape, gate_shape = (count, hidden), (scen, hidden)
+        gate_shape = (scen, hidden)
     shapes = [
         jax.ShapeDtypeStruct((toks, hidden, width), BF16),
-        jax.ShapeDtypeStruct(pre_shape, BF16),
+        jax.ShapeDtypeStruct((hidden // 128, count * toks, 128), F32),
         jax.ShapeDtypeStruct(gate_shape, F32),
     ]
+    out_specs = [anywhere, vmem, vmem]
+    if merge:
+        shapes.append(jax.ShapeDtypeStruct((count, toks, hidden), BF16))
+        out_specs.append(anywhere)
     if not t:
         shapes.append(jax.ShapeDtypeStruct((toks, width // parts), F32))
+        out_specs.append(vmem)
         scratch.append(pltpu.VMEM((shards[0].shape[1], 128), F32))
     return pl.pallas_call(
         functools.partial(token_kernel, t, at, parts, merge, sources),
         in_specs=specs,
-        out_specs=[anywhere, anywhere if merge else vmem] + [vmem] * (len(shapes) - 2),
+        out_specs=out_specs,
         scratch_shapes=scratch,
         out_shape=shapes,
         input_output_aliases=aliases,
@@ -460,7 +465,7 @@
         [v] for v in activations(0, pre_act, gates, scenario.reshape(1, -1), down_weight)
     ]
     hop(0, h[0])
-    hop(1, h[0])
+    hop(1, h[0], shards[2][1])
     hot, rest = hot[0], rest[0]
     more = activations(2, rest, gates, hot, down_weight)
     for have, new in zip((h, act, mul, held), more):
@@ -472,19 +477,19 @@
     hop(1, h[1])
     hot = after(hot, d_input)
 
-    down, done = None, []
+    down, rows, done = None, None, []
     homes = [(i, k) for i, v in enumerate(dz) for k in range(v.shape[0])]
     for t, (i, at) in enumerate(homes):
-        down, pre, gate, *more = token_step(
-            t, at, len(homes), sources, shards[i], held[t // 2], act[t // 2], mul[t // 2], h[t // 2], hot, down, done
+        down, rows, gate, *more = token_step(
+            t, at, len(homes), sources, shards[i], held[t // 2], act[t // 2], mul[t // 2], h[t // 2], hot, (down, rows), done
         )
-        done.append((pre, gate))
+        done.append(gate)
         if t == 0:
             gain_gradient = more[0]
             hop(2, gate)
         if t == 1:
             hop(3, gate)
-    return d_input, pre, down, gate, gain_gradient
+    return d_input, more[0], down, gate, gain_gradient
 
 
 def per_device(pre_norm, cotangent, gain, pre_act, gates, down_weight, scenario):

time: 58 us -> 57.4 us (0.990)
  waiting for transfers between devices: 7.05 us -> 5.02 us
  starting transfers between devices: 18.3 us -> 19.7 us
    ppermute x12, waiting for transfers between devices: 7.04 us -> 5.01 us  [hop(): lax.ppermute(after(last, *others) if others else last, 'dp', ring)]
    ppermute x12, starting transfers between devices: 16.4 us -> 18.2 us  [hop(): lax.ppermute(after(last, *others) if others else last, 'dp', ring)]
  transfers between devices with their start and end apart: 15 -> 15, of which waited for: 6 -> 4; matrix products, arithmetic and copies ran while one was open for 0% -> 0% of each run, Pallas kernels for 39% -> 40%
where the time goes in v3:
time: 57.4 us; the launch traced here: 57.3 us
  Pallas kernels  31.6 us (55%)
  starting transfers between devices  19.7 us (34%)
  waiting for transfers between devices  5.02 us (9%)
  between operations  0.9 us (2%)
    pallas_call x4, Pallas kernels, token_step(): pl.pallas_call(functools.partial(token_kernel, t, at, parts, merge, sourc...  18.7 us
    ppermute x12, starting transfers between devices, hop(): lax.ppermute(after(last, *others) if others else last, 'dp', ring)  18.2 us
    pallas_call x2, Pallas kernels, activations(): pl.pallas_call(functools.partial(act_kernel, parts, first, toks), in_spec...  8.55 us
    ppermute x12, waiting for transfers between devices, hop(): lax.ppermute(after(last, *others) if others else last, 'dp', ring)  5.01 us
    pallas_call x1, Pallas kernels, norm(): pl.pallas_call(functools.partial(norm_kernel, pieces, len(chunks)), out_s...  2.98 us
    ppermute x3, starting transfers between devices, swap(): lax.ppermute(v, 'tok', [(p, p ^ k + 1) for p in range(groups)])  1.56 us
    pallas_call x1, Pallas kernels, mix(): pl.pallas_call(functools.partial(mix_kernel, 1 + len(recv)), out_shape=ja...  1.34 us
  transfers between devices with their start and end apart: 15, of which 4 were waited for; matrix products, arithmetic and copies ran while one was open for 0% of the time, Pallas kernels for 40%

profile of v3, /device:TPU:0, one launch (start us, length us, event | category | flops | bytes accessed | tf_op | source)
XLA Modules:
  0.0 57.3 jit_solution(18414029880837030477)
XLA Ops:
  0.6 3.0 %norm.1 = (bf16[1,48,1792]{2,1,0:T(8,128)(2,1)S(1)}, bf16[1,48,1536]{2,1,0:T(8,128)(2,1)S(1)}, bf16[1,48,1536]{2,1,0:T(8,128)(2,1)S(1)}, bf16[1,48,1536]{2,1,0:T...) custom-call(bf16[48,4,1536]{2,1,0:T(4,128)(2,1)} %x_hbm.1, ...), custom_call_target="tpu_custom_call" | custom-call | tf_op jit(solution)/shard_map/norm/pallas_call | solution.py:115
  3.6 3.1 %collective-permute-start.9 = (bf16[1,48,1792]{2,1,0:T(8,128)(2,1)S(1)}, bf16[1,48,1792]{2,1,0:T(8,128)(2,1)S(1)}, u32[]{:S(2)}, u32[]{:S(2)}) collective-permute-start(bf16[1,48,1792]{2,1,0:T(8,128)(2,1)S(1)} %get-tuple-element.51.refs_3_.refs_0_), channel_id=1, source_target_pairs={{0,4},{4,12},{12,8},{8,0},{1,5},{5,13},{13,9},{9,1},{2,6},{6,14},{... | collective-permute-start | bytes 516104 | tf_op jit(solution)/shard_map/ppermute | solution.py:459
  6.7 2.6 %collective-permute-start.6 = (bf16[1,48,1536]{2,1,0:T(8,128)(2,1)S(1)}, bf16[1,48,1536]{2,1,0:T(8,128)(2,1)S(1)}, u32[]{:S(2)}, u32[]{:S(2)}) collective-permute-start(bf16[1,48,1536]{2,1,0:T(8,128)(2,1)S(1)} %get-tuple-element.53.refs_5_.refs_0_), channel_id=1, source_target_pairs={{0,4},{4,12},{12,8},{8,0},{1,5},{5,13},{13,9},{9,1},{2,6},{6,14},{... | collective-permute-start | bytes 442376 | tf_op jit(solution)/shard_map/ppermute | solution.py:459
  9.3 0.4 collective-permute-start.5
  9.7 4.6 %act.2 = (bf16[2,192,1536]{2,1,0:T(8,128)(2,1)S(1)}, f32[2,192,1536]{2,1,0:T(8,128)S(1)}, f32[2,192,1536]{2,1,0:T(8,128)S(1)}, bf16[2,1536,1536]{2,1,0:T(8,128)(...) custom-call(bf16[192,4,1536]{2,1,0:T(4,128)(2,1)} %source.1, f32[8,4,1536]{2,1,0:T(4,128)} %gates_hbm.3, ...), custom_call_target="tpu_custom_call" | custom-call | flops 1 | bytes 1 | tf_op jit(solution)/shard_map/act/pallas_call | solution.py:268
  14.4 0.1 collective-permute-start.10
  14.5 0.0 collective-permute-start
  14.5 1.6 %collective-permute-done.6.refs_1_ = bf16[1,48,1536]{2,1,0:T(8,128)(2,1)S(1)} collective-permute-done((bf16[1,48,1536]{2,1,0:T(8,128)(2,1)S(1)}, bf16[1,48,1536]{2,1,0:T(8,128)(2,1)S(1)}, u32[]{:S(2)}, u32[]{:S(2)}) %collective-permute-start.6) | collective-permute-done | bytes 147488 | tf_op jit(solution)/shard_map/ppermute | solution.py:459
  16.1 3.2 %collective-permute-done.5.refs_1_ = bf16[1,48,1536]{2,1,0:T(8,128)(2,1)S(1)} collective-permute-done((bf16[1,48,1536]{2,1,0:T(8,128)(2,1)S(1)}, bf16[1,48,1536]{2,1,0:T(8,128)(2,1)S(1)}, u32[]{:S(2)}, u32[]{:S(2)}) %collective-permute-start.5) | collective-permute-done | bytes 147488 | tf_op jit(solution)/shard_map/ppermute | solution.py:459
  19.2 1.2 %collective-permute-start.7 = (bf16[1,48,1536]{2,1,0:T(8,128)(2,1)S(1)}, bf16[1,48,1536]{2,1,0:T(8,128)(2,1)S(1)}, u32[]{:S(2)}, u32[]{:S(2)}) collective-permute-start(bf16[1,48,1536]{2,1,0:T(8,128)(2,1)S(1)} %collective-permute-done.5.refs_1_), channel_id=1, source_target_pairs={{0,4},{4,12},{12,8},{8,0},{1,5},{5,13},{13,9},{9,1},{2,6},{6,14},{... | collective-permute-start | bytes 442376 | tf_op jit(solution)/shard_map/ppermute | solution.py:459
  20.4 1.5 %collective-permute-start.1 = (bf16[4,48,384]{2,1,0:T(8,128)(2,1)S(1)}, bf16[4,48,384]{2,1,0:T(8,128)(2,1)S(1)}, u32[]{:S(2)}, u32[]{:S(2)}) collective-permute-start(bf16[4,48,384]{2,1,0:T(8,128)(2,1)S(1)} %get-tuple-element.47), channel_id=1, source_target_pairs={{0,2},{1,3},{2,0},{3,1},{4,6},{5,7},{6,4},{7,5},{8,10},{9,11},{10,... | collective-permute-start | bytes 442376 | tf_op jit(solution)/shard_map/ppermute | solution.py:445
  21.9 3.4 %collective-permute-start.3 = (bf16[1,48,1536]{2,1,0:T(8,128)(2,1)S(1)}, bf16[1,48,1536]{2,1,0:T(8,128)(2,1)S(1)}, u32[]{:S(2)}, u32[]{:S(2)}) collective-permute-start(bf16[1,48,1536]{2,1,0:T(8,128)(2,1)S(1)} %get-tuple-element.54.refs_6_.refs_0_), channel_id=1, source_target_pairs={{0,4},{4,12},{12,8},{8,0},{1,5},{5,13},{13,9},{9,1},{2,6},{6,14},{... | collective-permute-start | bytes 442376 | tf_op jit(solution)/shard_map/ppermute | solution.py:459
  25.3 0.0 collective-permute-done.10.refs_2_
  25.3 0.0 collective-permute-start.11
  25.3 0.0 collective-permute-start.2
  25.4 3.9 %act.3 = (bf16[2,192,1536]{2,1,0:T(8,128)(2,1)S(1)}, f32[2,192,1536]{2,1,0:T(8,128)S(1)}, f32[2,192,1536]{2,1,0:T(8,128)S(1)}, bf16[2,1536,1536]{2,1,0:T(8,128)(2,1)S(1)}) custom-call(f32[2,192,1536]{2,1,0:T(8,128)S(1)} %get-tuple-element.56.source, f32[8,4,1536]{2,1,0:T(4,128)} %gates_hbm.3, bf16[8,192]{1,0:T(8,128)(2,1)S(1)} %get-tuple-element.63.pick.refs_8_, ...), custom_call_target="tpu_custom_call" | custom-call | flops 1 | bytes 1 | tf_op jit(solution)/shard_map/act/pallas_call | solution.py:268
  29.3 0.0 collective-permute-done.7.refs_2_
  29.3 2.2 %collective-permute-start.13 = (bf16[1,48,1536]{2,1,0:T(8,128)(2,1)S(1)}, bf16[1,48,1536]{2,1,0:T(8,128)(2,1)S(1)}, u32[]{:S(2)}, u32[]{:S(2)}) collective-permute-start(bf16[1,48,1536]{2,1,0:T(8,128)(2,1)S(1)} %collective-permute-done.6.refs_1_), channel_id=1, source_target_pairs={{0,4},{4,12},{12,8},{8,0},{1,5},{5,13},{13,9},{9,1},{2,6},{6,14},{... | collective-permute-start | bytes 442376 | tf_op jit(solution)/shard_map/ppermute | solution.py:459
  31.5 0.1 collective-permute-start.8
  31.5 2.7 %collective-permute-start.4 = (bf16[1,48,1536]{2,1,0:T(8,128)(2,1)S(1)}, bf16[1,48,1536]{2,1,0:T(8,128)(2,1)S(1)}, u32[]{:S(2)}, u32[]{:S(2)}) collective-permute-start(bf16[1,48,1536]{2,1,0:T(8,128)(2,1)S(1)} %collective-permute-done.3.refs_1_), channel_id=1, source_target_pairs={{0,4},{4,12},{12,8},{8,0},{1,5},{5,13},{13,9},{9,1},{2,6},{6,14},{... | collective-permute-start | bytes 442376 | tf_op jit(solution)/shard_map/ppermute | solution.py:459
  34.2 0.0 collective-permute-done.2.refs_2_
  34.2 1.3 %mix.1 = bf16[48,4,1536]{2,1,0:T(4,128)(2,1)} custom-call(bf16[4,48,384]{2,1,0:T(8,128)(2,1)S(1)} %collective-permute-done.refs_0_, bf16[4,48,384]{2,1,0:T(8,128)(2,1)S(1)} %collective-permute-done.1.refs_1_, bf16[4,48,384]{2,1,0:T(8,128)(2,1)S(1)} %collective-permute-done.2.refs_2_, bf16[1,48,1792]{2,1,0:T(8,128)(2,1)S(1)} %get-tuple-element.51.refs_3_.refs_0_, ...), custom_call_target="tpu_custom_call" | custom-call | flops 1 | bytes 1 | tf_op jit(solution)/shard_map/mix/pallas_call | solution.py:162
  35.6 4.9 %token_.4 = (bf16[4,1536,1536]{2,1,0:T(8,128)(2,1)}, f32[12,768,128]{2,1,0:T(8,128)S(1)}, f32[8,1536]{1,0:T(8,128)S(1)}, f32[4,384]{1,0:T(4,128)}) custom-call(bf16[1,48,1792]{2,1,0:T(8,128)(2,1)S(1)} %get-tuple-element.51.refs_3_.refs_0_, bf16[1,48,1792]{2,1,0:T(8,128)(2,1)S(1)} %collective-permute-done.9.refs_1_, ...), custom_call_target="tpu_custom_call" | custom-call | flops 1 | bytes 1 | tf_op jit(solution)/shard_map/token/pallas_call | solution.py:412
  40.5 0.0 collective-permute-done.13.refs_2_
  40.5 0.5 collective-permute-start.14
  40.9 4.1 %token_.5 = (bf16[4,1536,1536]{2,1,0:T(8,128)(2,1)}, f32[12,768,128]{2,1,0:T(8,128)S(1)}, f32[8,1536]{1,0:T(8,128)S(1)}) custom-call(bf16[1,48,1536]{2,1,0:T(8,128)(2,1)S(1)} %get-tuple-element.52.refs_4_.refs_0_, bf16[1,48,1536]{2,1,0:T(8,128)(2,1)S(1)} %collective-permute-done.5.refs_1_, ...), custom_call_target="tpu_custom_call", output_to_operand_aliasing={{0}: (9, {}), {1}: (10, {})} | custom-call | flops 1 | bytes 1 | tf_op jit(solution)/shard_map/token/pallas_call | solution.py:412
  45.0 0.0 collective-permute-done.4.refs_2_
  45.0 2.0 %collective-permute-start.12 = (bf16[1,48,1536]{2,1,0:T(8,128)(2,1)S(1)}, bf16[1,48,1536]{2,1,0:T(8,128)(2,1)S(1)}, u32[]{:S(2)}, u32[]{:S(2)}) collective-permute-start(bf16[1,48,1536]{2,1,0:T(8,128)(2,1)S(1)} %collective-permute-done.4.refs_2_), channel_id=1, source_target_pairs={{0,4},{4,12},{12,8},{8,0},{1,5},{5,13},{13,9},{9,1},{2,6},{6,14},{... | collective-permute-start | bytes 442376 | tf_op jit(solution)/shard_map/ppermute | solution.py:459
  47.0 0.1 collective-permute-done.14.refs_3_
  47.1 4.0 %token_.6 = (bf16[4,1536,1536]{2,1,0:T(8,128)(2,1)}, f32[12,768,128]{2,1,0:T(8,128)S(1)}, f32[8,1536]{1,0:T(8,128)S(1)}) custom-call(bf16[1,48,1536]{2,1,0:T(8,128)(2,1)S(1)} %get-tuple-element.53.refs_5_.refs_0_, bf16[1,48,1536]{2,1,0:T(8,128)(2,1)S(1)} %collective-permute-done.6.refs_1_, ...), custom_call_target="tpu_custom_call", output_to_operand_aliasing={{0}: (9, {}), {1}: (10, {})} | custom-call | flops 1 | bytes 1 | tf_op jit(solution)/shard_map/token/pallas_call | solution.py:412
  51.2 0.1 collective-permute-done.12.refs_3_
  51.4 5.8 %token_.7 = (bf16[4,1536,1536]{2,1,0:T(8,128)(2,1)}, f32[12,768,128]{2,1,0:T(8,128)S(1)}, f32[8,4,1536]{2,1,0:T(4,128)}, bf16[192,4,1536]{2,1,0:T(4,128)(2,1)}) custom-call(bf16[1,48,1536]{2,1,0:T(8,128)(2,1)S(1)} %get-tuple-element.54.refs_6_.refs_0_, ...), custom_call_target="tpu_custom_call", output_to_operand_aliasing={{0}: (9, {}), {1}: (10, {})} | custom-call | flops 1 | bytes 1 | tf_op jit(solution)/shard_map/token/pallas_call | solution.py:412
  (6 shorter events, 0.0 us)
Async XLA Ops:
  3.6 10.7 %collective-permute-start.9 = (bf16[1,48,1792]{2,1,0:T(8,128)(2,1)S(1)}, bf16[1,48,1792]{2,1,0:T(8,128)(2,1)S(1)}, u32[]{:S(2)}, u32[]{:S(2)}) collective-permute-start(bf16[1,48,1792]{2,1,0:T(8,128)(2,1)S(1)} %get-tuple-element.51.refs_3_.refs_0_), channel_id=1, source_target_pairs={{0,4},{4,12},{12,8},{8,0},{1,5},{5,13},{13,9},{9,1},{2,6},{6,14},{... | collective-permute-start | bytes 516104 | tf_op jit(solution)/shard_map/ppermute | solution.py:459
  6.7 9.4 %collective-permute-start.6 = (bf16[1,48,1536]{2,1,0:T(8,128)(2,1)S(1)}, bf16[1,48,1536]{2,1,0:T(8,128)(2,1)S(1)}, u32[]{:S(2)}, u32[]{:S(2)}) collective-permute-start(bf16[1,48,1536]{2,1,0:T(8,128)(2,1)S(1)} %get-tuple-element.53.refs_5_.refs_0_), channel_id=1, source_target_pairs={{0,4},{4,12},{12,8},{8,0},{1,5},{5,13},{13,9},{9,1},{2,6},{6,14},{... | collective-permute-start | bytes 442376 | tf_op jit(solution)/shard_map/ppermute | solution.py:459
  9.3 9.9 %collective-permute-start.5 = (bf16[1,48,1536]{2,1,0:T(8,128)(2,1)S(1)}, bf16[1,48,1536]{2,1,0:T(8,128)(2,1)S(1)}, u32[]{:S(2)}, u32[]{:S(2)}) collective-permute-start(bf16[1,48,1536]{2,1,0:T(8,128)(2,1)S(1)} %get-tuple-element.52.refs_4_.refs_0_), channel_id=1, source_target_pairs={{0,4},{4,12},{12,8},{8,0},{1,5},{5,13},{13,9},{9,1},{2,6},{6,14},{... | collective-permute-start | bytes 442376 | tf_op jit(solution)/shard_map/ppermute | solution.py:459
  14.4 10.9 %collective-permute-start.10 = (bf16[1,48,1792]{2,1,0:T(8,128)(2,1)S(1)}, bf16[1,48,1792]{2,1,0:T(8,128)(2,1)S(1)}, u32[]{:S(2)}, u32[]{:S(2)}) collective-permute-start(bf16[1,48,1792]{2,1,0:T(8,128)(2,1)S(1)} %collective-permute-done.9.refs_1_), channel_id=1, source_target_pairs={{0,4},{4,12},{12,8},{8,0},{1,5},{5,13},{13,9},{9,1},{2,6},{6,14},{... | collective-permute-start | bytes 516104 | tf_op jit(solution)/shard_map/ppermute | solution.py:459
  14.5 10.8 %collective-permute-start = (bf16[4,48,384]{2,1,0:T(8,128)(2,1)S(1)}, bf16[4,48,384]{2,1,0:T(8,128)(2,1)S(1)}, u32[]{:S(2)}, u32[]{:S(2)}) collective-permute-start(bf16[4,48,384]{2,1,0:T(8,128)(2,1)S(1)} %get-tuple-element.44), channel_id=1, source_target_pairs={{0,1},{1,0},{2,3},{3,2},{4,5},{5,4},{6,7},{7,6},{8,9},{9,8},{10,11... | collective-permute-start | bytes 442376 | tf_op jit(solution)/shard_map/ppermute | solution.py:445
  19.2 10.1 %collective-permute-start.7 = (bf16[1,48,1536]{2,1,0:T(8,128)(2,1)S(1)}, bf16[1,48,1536]{2,1,0:T(8,128)(2,1)S(1)}, u32[]{:S(2)}, u32[]{:S(2)}) collective-permute-start(bf16[1,48,1536]{2,1,0:T(8,128)(2,1)S(1)} %collective-permute-done.5.refs_1_), channel_id=1, source_target_pairs={{0,4},{4,12},{12,8},{8,0},{1,5},{5,13},{13,9},{9,1},{2,6},{6,14},{... | collective-permute-start | bytes 442376 | tf_op jit(solution)/shard_map/ppermute | solution.py:459
  20.4 11.1 %collective-permute-start.1 = (bf16[4,48,384]{2,1,0:T(8,128)(2,1)S(1)}, bf16[4,48,384]{2,1,0:T(8,128)(2,1)S(1)}, u32[]{:S(2)}, u32[]{:S(2)}) collective-permute-start(bf16[4,48,384]{2,1,0:T(8,128)(2,1)S(1)} %get-tuple-element.47), channel_id=1, source_target_pairs={{0,2},{1,3},{2,0},{3,1},{4,6},{5,7},{6,4},{7,5},{8,10},{9,11},{10,... | collective-permute-start | bytes 442376 | tf_op jit(solution)/shard_map/ppermute | solution.py:445
  21.9 9.7 %collective-permute-start.3 = (bf16[1,48,1536]{2,1,0:T(8,128)(2,1)S(1)}, bf16[1,48,1536]{2,1,0:T(8,128)(2,1)S(1)}, u32[]{:S(2)}, u32[]{:S(2)}) collective-permute-start(bf16[1,48,1536]{2,1,0:T(8,128)(2,1)S(1)} %get-tuple-element.54.refs_6_.refs_0_), channel_id=1, source_target_pairs={{0,4},{4,12},{12,8},{8,0},{1,5},{5,13},{13,9},{9,1},{2,6},{6,14},{... | collective-permute-start | bytes 442376 | tf_op jit(solution)/shard_map/ppermute | solution.py:459
  25.3 10.3 %collective-permute-start.11 = (bf16[1,48,1792]{2,1,0:T(8,128)(2,1)S(1)}, bf16[1,48,1792]{2,1,0:T(8,128)(2,1)S(1)}, u32[]{:S(2)}, u32[]{:S(2)}) collective-permute-start(bf16[1,48,1792]{2,1,0:T(8,128)(2,1)S(1)} %collective-permute-done.10.refs_2_), channel_id=1, source_target_pairs={{0,4},{4,12},{12,8},{8,0},{1,5},{5,13},{13,9},{9,1},{2,6},{6,14},{... | collective-permute-start | bytes 516104 | tf_op jit(solution)/shard_map/ppermute | solution.py:459
  25.3 8.9 %collective-permute-start.2 = (bf16[4,48,384]{2,1,0:T(8,128)(2,1)S(1)}, bf16[4,48,384]{2,1,0:T(8,128)(2,1)S(1)}, u32[]{:S(2)}, u32[]{:S(2)}) collective-permute-start(bf16[4,48,384]{2,1,0:T(8,128)(2,1)S(1)} %get-tuple-element.49), channel_id=1, source_target_pairs={{0,3},{1,2},{2,1},{3,0},{4,7},{5,6},{6,5},{7,4},{8,11},{9,10},{10,... | collective-permute-start | bytes 442376 | tf_op jit(solution)/shard_map/ppermute | solution.py:445
  29.3 11.2 %collective-permute-start.13 = (bf16[1,48,1536]{2,1,0:T(8,128)(2,1)S(1)}, bf16[1,48,1536]{2,1,0:T(8,128)(2,1)S(1)}, u32[]{:S(2)}, u32[]{:S(2)}) collective-permute-start(bf16[1,48,1536]{2,1,0:T(8,128)(2,1)S(1)} %collective-permute-done.6.refs_1_), channel_id=1, source_target_pairs={{0,4},{4,12},{12,8},{8,0},{1,5},{5,13},{13,9},{9,1},{2,6},{6,14},{... | collective-permute-start | bytes 442376 | tf_op jit(solution)/shard_map/ppermute | solution.py:459
  31.5 9.5 %collective-permute-start.8 = (bf16[1,48,1536]{2,1,0:T(8,128)(2,1)S(1)}, bf16[1,48,1536]{2,1,0:T(8,128)(2,1)S(1)}, u32[]{:S(2)}, u32[]{:S(2)}) collective-permute-start(bf16[1,48,1536]{2,1,0:T(8,128)(2,1)S(1)} %collective-permute-done.7.refs_2_), channel_id=1, source_target_pairs={{0,4},{4,12},{12,8},{8,0},{1,5},{5,13},{13,9},{9,1},{2,6},{6,14},{... | collective-permute-start | bytes 442376 | tf_op jit(solution)/shard_map/ppermute | solution.py:459
  31.5 13.5 %collective-permute-start.4 = (bf16[1,48,1536]{2,1,0:T(8,128)(2,1)S(1)}, bf16[1,48,1536]{2,1,0:T(8,128)(2,1)S(1)}, u32[]{:S(2)}, u32[]{:S(2)}) collective-permute-start(bf16[1,48,1536]{2,1,0:T(8,128)(2,1)S(1)} %collective-permute-done.3.refs_1_), channel_id=1, source_target_pairs={{0,4},{4,12},{12,8},{8,0},{1,5},{5,13},{13,9},{9,1},{2,6},{6,14},{... | collective-permute-start | bytes 442376 | tf_op jit(solution)/shard_map/ppermute | solution.py:459
  40.5 6.7 %collective-permute-start.14 = (bf16[1,48,1536]{2,1,0:T(8,128)(2,1)S(1)}, bf16[1,48,1536]{2,1,0:T(8,128)(2,1)S(1)}, u32[]{:S(2)}, u32[]{:S(2)}) collective-permute-start(bf16[1,48,1536]{2,1,0:T(8,128)(2,1)S(1)} %collective-permute-done.13.refs_2_), channel_id=1, source_target_pairs={{0,4},{4,12},{12,8},{8,0},{1,5},{5,13},{13,9},{9,1},{2,6},{6,14},{... | collective-permute-start | bytes 442376 | tf_op jit(solution)/shard_map/ppermute | solution.py:459
  45.0 6.3 %collective-permute-start.12 = (bf16[1,48,1536]{2,1,0:T(8,128)(2,1)S(1)}, bf16[1,48,1536]{2,1,0:T(8,128)(2,1)S(1)}, u32[]{:S(2)}, u32[]{:S(2)}) collective-permute-start(bf16[1,48,1536]{2,1,0:T(8,128)(2,1)S(1)} %collective-permute-done.4.refs_2_), channel_id=1, source_target_pairs={{0,4},{4,12},{12,8},{8,0},{1,5},{5,13},{13,9},{9,1},{2,6},{6,14},{... | collective-permute-start | bytes 442376 | tf_op jit(solution)/shard_map/ppermute | solution.py:459

commit v4 on v3

--- a/solution.py
+++ b/solution.py
@@ -471,10 +471,10 @@
     for have, new in zip((h, act, mul, held), more):
         have.append(new)
     d_input = mix([after(r, h[0]) for r in recv], dz, down_weight.shape[2])
-    hop(2)
+    hop(2, h[1])
     hop(3)
     hop(0)
-    hop(1, h[1])
+    hop(1)
     hot = after(hot, d_input)
 
     down, rows, done = None, None, []

time: 57.4 us -> 57.2 us (level)
  waiting for transfers between devices: 5.02 us -> 3.04 us
  starting transfers between devices: 19.7 us -> 21.5 us
    ppermute x12, waiting for transfers between devices: 5.01 us -> 3.04 us  [hop(): lax.ppermute(after(last, *others) if others else last, 'dp', ring)]
    ppermute x12, starting transfers between devices: 18.2 us -> 19.7 us  [hop(): lax.ppermute(after(last, *others) if others else last, 'dp', ring)]
  transfers between devices with their start and end apart: 15 -> 15, of which waited for: 4 -> 1; matrix products, arithmetic and copies ran while one was open for 0% -> 0% of each run, Pallas kernels for 40% -> 40%
where the time goes in v4:
time: 57.2 us; the launch traced here: 57 us
  Pallas kernels  31.6 us (55%)
  starting transfers between devices  21.5 us (38%)
  waiting for transfers between devices  3.04 us (5%)
  between operations  0.89 us (2%)
    ppermute x12, starting transfers between devices, hop(): lax.ppermute(after(last, *others) if others else last, 'dp', ring)  19.7 us
    pallas_call x4, Pallas kernels, token_step(): pl.pallas_call(functools.partial(token_kernel, t, at, parts, merge, sourc...  18.7 us
    pallas_call x2, Pallas kernels, activations(): pl.pallas_call(functools.partial(act_kernel, parts, first, toks), in_spec...  8.55 us
    ppermute x12, waiting for transfers between devices, hop(): lax.ppermute(after(last, *others) if others else last, 'dp', ring)  3.04 us
    pallas_call x1, Pallas kernels, norm(): pl.pallas_call(functools.partial(norm_kernel, pieces, len(chunks)), out_s...  2.98 us
    ppermute x3, starting transfers between devices, swap(): lax.ppermute(v, 'tok', [(p, p ^ k + 1) for p in range(groups)])  1.76 us
    pallas_call x1, Pallas kernels, mix(): pl.pallas_call(functools.partial(mix_kernel, 1 + len(recv)), out_shape=ja...  1.34 us
  transfers between devices with their start and end apart: 15, of which 1 were waited for; matrix products, arithmetic and copies ran while one was open for 0% of the time, Pallas kernels for 40%

profile of v4, /device:TPU:0, one launch (start us, length us, event | category | flops | bytes accessed | tf_op | source)
XLA Modules:
  0.0 57.0 jit_solution(12387289810300642095)
XLA Ops:
  0.6 3.0 %norm.1 = (bf16[1,48,1792]{2,1,0:T(8,128)(2,1)S(1)}, bf16[1,48,1536]{2,1,0:T(8,128)(2,1)S(1)}, bf16[1,48,1536]{2,1,0:T(8,128)(2,1)S(1)}, bf16[1,48,1536]{2,1,0:T...) custom-call(bf16[48,4,1536]{2,1,0:T(4,128)(2,1)} %x_hbm.1, ...), custom_call_target="tpu_custom_call" | custom-call | tf_op jit(solution)/shard_map/norm/pallas_call | solution.py:115
  3.6 3.1 %collective-permute-start.9 = (bf16[1,48,1792]{2,1,0:T(8,128)(2,1)S(1)}, bf16[1,48,1792]{2,1,0:T(8,128)(2,1)S(1)}, u32[]{:S(2)}, u32[]{:S(2)}) collective-permute-start(bf16[1,48,1792]{2,1,0:T(8,128)(2,1)S(1)} %get-tuple-element.51.refs_3_.refs_0_), channel_id=1, source_target_pairs={{0,4},{4,12},{12,8},{8,0},{1,5},{5,13},{13,9},{9,1},{2,6},{6,14},{... | collective-permute-start | bytes 516104 | tf_op jit(solution)/shard_map/ppermute | solution.py:459
  6.7 2.6 %collective-permute-start.5 = (bf16[1,48,1536]{2,1,0:T(8,128)(2,1)S(1)}, bf16[1,48,1536]{2,1,0:T(8,128)(2,1)S(1)}, u32[]{:S(2)}, u32[]{:S(2)}) collective-permute-start(bf16[1,48,1536]{2,1,0:T(8,128)(2,1)S(1)} %get-tuple-element.52.refs_4_.refs_0_), channel_id=1, source_target_pairs={{0,4},{4,12},{12,8},{8,0},{1,5},{5,13},{13,9},{9,1},{2,6},{6,14},{... | collective-permute-start | bytes 442376 | tf_op jit(solution)/shard_map/ppermute | solution.py:459
  9.3 0.4 collective-permute-start.6
  9.7 4.6 %act.2 = (bf16[2,192,1536]{2,1,0:T(8,128)(2,1)S(1)}, f32[2,192,1536]{2,1,0:T(8,128)S(1)}, f32[2,192,1536]{2,1,0:T(8,128)S(1)}, bf16[2,1536,1536]{2,1,0:T(8,128)(...) custom-call(bf16[192,4,1536]{2,1,0:T(4,128)(2,1)} %source.1, f32[8,4,1536]{2,1,0:T(4,128)} %gates_hbm.3, ...), custom_call_target="tpu_custom_call" | custom-call | flops 1 | bytes 1 | tf_op jit(solution)/shard_map/act/pallas_call | solution.py:268
  14.4 0.0 collective-permute-done.9.refs_1_
  14.4 0.1 collective-permute-start.10
  14.5 0.0 collective-permute-start
  14.5 1.7 %collective-permute-start.1 = (bf16[4,48,384]{2,1,0:T(8,128)(2,1)S(1)}, bf16[4,48,384]{2,1,0:T(8,128)(2,1)S(1)}, u32[]{:S(2)}, u32[]{:S(2)}) collective-permute-start(bf16[4,48,384]{2,1,0:T(8,128)(2,1)S(1)} %get-tuple-element.47), channel_id=1, source_target_pairs={{0,2},{1,3},{2,0},{3,1},{4,6},{5,7},{6,4},{7,5},{8,10},{9,11},{10,... | collective-permute-start | bytes 442376 | tf_op jit(solution)/shard_map/ppermute | solution.py:445
  16.3 3.0 %collective-permute-done.6.refs_1_ = bf16[1,48,1536]{2,1,0:T(8,128)(2,1)S(1)} collective-permute-done((bf16[1,48,1536]{2,1,0:T(8,128)(2,1)S(1)}, bf16[1,48,1536]{2,1,0:T(8,128)(2,1)S(1)}, u32[]{:S(2)}, u32[]{:S(2)}) %collective-permute-start.6) | collective-permute-done | bytes 147488 | tf_op jit(solution)/shard_map/ppermute | solution.py:459
  19.2 1.2 %collective-permute-start.7 = (bf16[1,48,1536]{2,1,0:T(8,128)(2,1)S(1)}, bf16[1,48,1536]{2,1,0:T(8,128)(2,1)S(1)}, u32[]{:S(2)}, u32[]{:S(2)}) collective-permute-start(bf16[1,48,1536]{2,1,0:T(8,128)(2,1)S(1)} %collective-permute-done.5.refs_1_), channel_id=1, source_target_pairs={{0,4},{4,12},{12,8},{8,0},{1,5},{5,13},{13,9},{9,1},{2,6},{6,14},{... | collective-permute-start | bytes 442376 | tf_op jit(solution)/shard_map/ppermute | solution.py:459
  20.4 3.4 %collective-permute-start.3 = (bf16[1,48,1536]{2,1,0:T(8,128)(2,1)S(1)}, bf16[1,48,1536]{2,1,0:T(8,128)(2,1)S(1)}, u32[]{:S(2)}, u32[]{:S(2)}) collective-permute-start(bf16[1,48,1536]{2,1,0:T(8,128)(2,1)S(1)} %get-tuple-element.54.refs_6_.refs_0_), channel_id=1, source_target_pairs={{0,4},{4,12},{12,8},{8,0},{1,5},{5,13},{13,9},{9,1},{2,6},{6,14},{... | collective-permute-start | bytes 442376 | tf_op jit(solution)/shard_map/ppermute | solution.py:459
  23.8 0.3 collective-permute-start.11
  24.1 3.9 %act.3 = (bf16[2,192,1536]{2,1,0:T(8,128)(2,1)S(1)}, f32[2,192,1536]{2,1,0:T(8,128)S(1)}, f32[2,192,1536]{2,1,0:T(8,128)S(1)}, bf16[2,1536,1536]{2,1,0:T(8,128)(2,1)S(1)}) custom-call(f32[2,192,1536]{2,1,0:T(8,128)S(1)} %get-tuple-element.66.source, f32[8,4,1536]{2,1,0:T(4,128)} %gates_hbm.3, bf16[8,192]{1,0:T(8,128)(2,1)S(1)} %get-tuple-element.60.refs_8_.pick, ...), custom_call_target="tpu_custom_call" | custom-call | flops 1 | bytes 1 | tf_op jit(solution)/shard_map/act/pallas_call | solution.py:268
  28.0 0.0 collective-permute-done.1.refs_1_
  28.0 3.4 %collective-permute-start.13 = (bf16[1,48,1536]{2,1,0:T(8,128)(2,1)S(1)}, bf16[1,48,1536]{2,1,0:T(8,128)(2,1)S(1)}, u32[]{:S(2)}, u32[]{:S(2)}) collective-permute-start(bf16[1,48,1536]{2,1,0:T(8,128)(2,1)S(1)} %collective-permute-done.6.refs_1_), channel_id=1, source_target_pairs={{0,4},{4,12},{12,8},{8,0},{1,5},{5,13},{13,9},{9,1},{2,6},{6,14},{... | collective-permute-start | bytes 442376 | tf_op jit(solution)/shard_map/ppermute | solution.py:459
  31.5 0.0 collective-permute-done.7.refs_2_
  31.5 0.1 collective-permute-start.8
  31.5 0.0 collective-permute-done.3.refs_1_
  31.5 1.2 %collective-permute-start.4 = (bf16[1,48,1536]{2,1,0:T(8,128)(2,1)S(1)}, bf16[1,48,1536]{2,1,0:T(8,128)(2,1)S(1)}, u32[]{:S(2)}, u32[]{:S(2)}) collective-permute-start(bf16[1,48,1536]{2,1,0:T(8,128)(2,1)S(1)} %collective-permute-done.3.refs_1_), channel_id=1, source_target_pairs={{0,4},{4,12},{12,8},{8,0},{1,5},{5,13},{13,9},{9,1},{2,6},{6,14},{... | collective-permute-start | bytes 442376 | tf_op jit(solution)/shard_map/ppermute | solution.py:459
  32.7 0.0 collective-permute-done.2.refs_2_
  32.7 1.3 %mix.1 = bf16[48,4,1536]{2,1,0:T(4,128)(2,1)} custom-call(bf16[4,48,384]{2,1,0:T(8,128)(2,1)S(1)} %collective-permute-done.refs_0_, bf16[4,48,384]{2,1,0:T(8,128)(2,1)S(1)} %collective-permute-done.1.refs_1_, bf16[4,48,384]{2,1,0:T(8,128)(2,1)S(1)} %collective-permute-done.2.refs_2_, bf16[1,48,1792]{2,1,0:T(8,128)(2,1)S(1)} %get-tuple-element.51.refs_3_.refs_0_, ...), custom_call_target="tpu_custom_call" | custom-call | flops 1 | bytes 1 | tf_op jit(solution)/shard_map/mix/pallas_call | solution.py:162
  34.1 4.9 %token_.4 = (bf16[4,1536,1536]{2,1,0:T(8,128)(2,1)}, f32[12,768,128]{2,1,0:T(8,128)S(1)}, f32[8,1536]{1,0:T(8,128)S(1)}, f32[4,384]{1,0:T(4,128)}) custom-call(bf16[1,48,1792]{2,1,0:T(8,128)(2,1)S(1)} %get-tuple-element.51.refs_3_.refs_0_, bf16[1,48,1792]{2,1,0:T(8,128)(2,1)S(1)} %collective-permute-done.9.refs_1_, ...), custom_call_target="tpu_custom_call" | custom-call | flops 1 | bytes 1 | tf_op jit(solution)/shard_map/token/pallas_call | solution.py:412
  39.0 0.0 collective-permute-done.13.refs_2_
  39.0 2.0 %collective-permute-start.14 = (bf16[1,48,1536]{2,1,0:T(8,128)(2,1)S(1)}, bf16[1,48,1536]{2,1,0:T(8,128)(2,1)S(1)}, u32[]{:S(2)}, u32[]{:S(2)}) collective-permute-start(bf16[1,48,1536]{2,1,0:T(8,128)(2,1)S(1)} %collective-permute-done.13.refs_2_), channel_id=1, source_target_pairs={{0,4},{4,12},{12,8},{8,0},{1,5},{5,13},{13,9},{9,1},{2,6},{6,14},{... | collective-permute-start | bytes 442376 | tf_op jit(solution)/shard_map/ppermute | solution.py:459
  40.9 0.0 collective-permute-done.8.refs_3_
  40.9 4.1 %token_.5 = (bf16[4,1536,1536]{2,1,0:T(8,128)(2,1)}, f32[12,768,128]{2,1,0:T(8,128)S(1)}, f32[8,1536]{1,0:T(8,128)S(1)}) custom-call(bf16[1,48,1536]{2,1,0:T(8,128)(2,1)S(1)} %get-tuple-element.52.refs_4_.refs_0_, bf16[1,48,1536]{2,1,0:T(8,128)(2,1)S(1)} %collective-permute-done.5.refs_1_, ...), custom_call_target="tpu_custom_call", output_to_operand_aliasing={{0}: (9, {}), {1}: (10, {})} | custom-call | flops 1 | bytes 1 | tf_op jit(solution)/shard_map/token/pallas_call | solution.py:412
  45.0 0.0 collective-permute-done.4.refs_2_
  45.0 2.0 %collective-permute-start.12 = (bf16[1,48,1536]{2,1,0:T(8,128)(2,1)S(1)}, bf16[1,48,1536]{2,1,0:T(8,128)(2,1)S(1)}, u32[]{:S(2)}, u32[]{:S(2)}) collective-permute-start(bf16[1,48,1536]{2,1,0:T(8,128)(2,1)S(1)} %collective-permute-done.4.refs_2_), channel_id=1, source_target_pairs={{0,4},{4,12},{12,8},{8,0},{1,5},{5,13},{13,9},{9,1},{2,6},{6,14},{... | collective-permute-start | bytes 442376 | tf_op jit(solution)/shard_map/ppermute | solution.py:459
  47.0 4.1 %token_.6 = (bf16[4,1536,1536]{2,1,0:T(8,128)(2,1)}, f32[12,768,128]{2,1,0:T(8,128)S(1)}, f32[8,1536]{1,0:T(8,128)S(1)}) custom-call(bf16[1,48,1536]{2,1,0:T(8,128)(2,1)S(1)} %get-tuple-element.53.refs_5_.refs_0_, bf16[1,48,1536]{2,1,0:T(8,128)(2,1)S(1)} %collective-permute-done.6.refs_1_, ...), custom_call_target="tpu_custom_call", output_to_operand_aliasing={{0}: (9, {}), {1}: (10, {})} | custom-call | flops 1 | bytes 1 | tf_op jit(solution)/shard_map/token/pallas_call | solution.py:412
  51.1 0.0 collective-permute-done.12.refs_3_
  51.1 5.8 %token_.7 = (bf16[4,1536,1536]{2,1,0:T(8,128)(2,1)}, f32[12,768,128]{2,1,0:T(8,128)S(1)}, f32[8,4,1536]{2,1,0:T(4,128)}, bf16[192,4,1536]{2,1,0:T(4,128)(2,1)}) custom-call(bf16[1,48,1536]{2,1,0:T(8,128)(2,1)S(1)} %get-tuple-element.54.refs_6_.refs_0_, ...), custom_call_target="tpu_custom_call", output_to_operand_aliasing={{0}: (9, {}), {1}: (10, {})} | custom-call | flops 1 | bytes 1 | tf_op jit(solution)/shard_map/token/pallas_call | solution.py:412
  (6 shorter events, 0.0 us)
Async XLA Ops:
  3.6 10.7 %collective-permute-start.9 = (bf16[1,48,1792]{2,1,0:T(8,128)(2,1)S(1)}, bf16[1,48,1792]{2,1,0:T(8,128)(2,1)S(1)}, u32[]{:S(2)}, u32[]{:S(2)}) collective-permute-start(bf16[1,48,1792]{2,1,0:T(8,128)(2,1)S(1)} %get-tuple-element.51.refs_3_.refs_0_), channel_id=1, source_target_pairs={{0,4},{4,12},{12,8},{8,0},{1,5},{5,13},{13,9},{9,1},{2,6},{6,14},{... | collective-permute-start | bytes 516104 | tf_op jit(solution)/shard_map/ppermute | solution.py:459
  6.7 9.6 %collective-permute-start.5 = (bf16[1,48,1536]{2,1,0:T(8,128)(2,1)S(1)}, bf16[1,48,1536]{2,1,0:T(8,128)(2,1)S(1)}, u32[]{:S(2)}, u32[]{:S(2)}) collective-permute-start(bf16[1,48,1536]{2,1,0:T(8,128)(2,1)S(1)} %get-tuple-element.52.refs_4_.refs_0_), channel_id=1, source_target_pairs={{0,4},{4,12},{12,8},{8,0},{1,5},{5,13},{13,9},{9,1},{2,6},{6,14},{... | collective-permute-start | bytes 442376 | tf_op jit(solution)/shard_map/ppermute | solution.py:459
  9.3 9.9 %collective-permute-start.6 = (bf16[1,48,1536]{2,1,0:T(8,128)(2,1)S(1)}, bf16[1,48,1536]{2,1,0:T(8,128)(2,1)S(1)}, u32[]{:S(2)}, u32[]{:S(2)}) collective-permute-start(bf16[1,48,1536]{2,1,0:T(8,128)(2,1)S(1)} %get-tuple-element.53.refs_5_.refs_0_), channel_id=1, source_target_pairs={{0,4},{4,12},{12,8},{8,0},{1,5},{5,13},{13,9},{9,1},{2,6},{6,14},{... | collective-permute-start | bytes 442376 | tf_op jit(solution)/shard_map/ppermute | solution.py:459
  14.4 9.4 %collective-permute-start.10 = (bf16[1,48,1792]{2,1,0:T(8,128)(2,1)S(1)}, bf16[1,48,1792]{2,1,0:T(8,128)(2,1)S(1)}, u32[]{:S(2)}, u32[]{:S(2)}) collective-permute-start(bf16[1,48,1792]{2,1,0:T(8,128)(2,1)S(1)} %collective-permute-done.9.refs_1_), channel_id=1, source_target_pairs={{0,4},{4,12},{12,8},{8,0},{1,5},{5,13},{13,9},{9,1},{2,6},{6,14},{... | collective-permute-start | bytes 516104 | tf_op jit(solution)/shard_map/ppermute | solution.py:459
  14.5 9.6 %collective-permute-start = (bf16[4,48,384]{2,1,0:T(8,128)(2,1)S(1)}, bf16[4,48,384]{2,1,0:T(8,128)(2,1)S(1)}, u32[]{:S(2)}, u32[]{:S(2)}) collective-permute-start(bf16[4,48,384]{2,1,0:T(8,128)(2,1)S(1)} %get-tuple-element.44), channel_id=1, source_target_pairs={{0,1},{1,0},{2,3},{3,2},{4,5},{5,4},{6,7},{7,6},{8,9},{9,8},{10,11... | collective-permute-start | bytes 442376 | tf_op jit(solution)/shard_map/ppermute | solution.py:445
  14.5 13.5 %collective-permute-start.1 = (bf16[4,48,384]{2,1,0:T(8,128)(2,1)S(1)}, bf16[4,48,384]{2,1,0:T(8,128)(2,1)S(1)}, u32[]{:S(2)}, u32[]{:S(2)}) collective-permute-start(bf16[4,48,384]{2,1,0:T(8,128)(2,1)S(1)} %get-tuple-element.47), channel_id=1, source_target_pairs={{0,2},{1,3},{2,0},{3,1},{4,6},{5,7},{6,4},{7,5},{8,10},{9,11},{10,... | collective-permute-start | bytes 442376 | tf_op jit(solution)/shard_map/ppermute | solution.py:445
  19.2 12.2 %collective-permute-start.7 = (bf16[1,48,1536]{2,1,0:T(8,128)(2,1)S(1)}, bf16[1,48,1536]{2,1,0:T(8,128)(2,1)S(1)}, u32[]{:S(2)}, u32[]{:S(2)}) collective-permute-start(bf16[1,48,1536]{2,1,0:T(8,128)(2,1)S(1)} %collective-permute-done.5.refs_1_), channel_id=1, source_target_pairs={{0,4},{4,12},{12,8},{8,0},{1,5},{5,13},{13,9},{9,1},{2,6},{6,14},{... | collective-permute-start | bytes 442376 | tf_op jit(solution)/shard_map/ppermute | solution.py:459
  20.4 11.2 %collective-permute-start.3 = (bf16[1,48,1536]{2,1,0:T(8,128)(2,1)S(1)}, bf16[1,48,1536]{2,1,0:T(8,128)(2,1)S(1)}, u32[]{:S(2)}, u32[]{:S(2)}) collective-permute-start(bf16[1,48,1536]{2,1,0:T(8,128)(2,1)S(1)} %get-tuple-element.54.refs_6_.refs_0_), channel_id=1, source_target_pairs={{0,4},{4,12},{12,8},{8,0},{1,5},{5,13},{13,9},{9,1},{2,6},{6,14},{... | collective-permute-start | bytes 442376 | tf_op jit(solution)/shard_map/ppermute | solution.py:459
  23.8 10.3 %collective-permute-start.11 = (bf16[1,48,1792]{2,1,0:T(8,128)(2,1)S(1)}, bf16[1,48,1792]{2,1,0:T(8,128)(2,1)S(1)}, u32[]{:S(2)}, u32[]{:S(2)}) collective-permute-start(bf16[1,48,1792]{2,1,0:T(8,128)(2,1)S(1)} %collective-permute-done.10.refs_2_), channel_id=1, source_target_pairs={{0,4},{4,12},{12,8},{8,0},{1,5},{5,13},{13,9},{9,1},{2,6},{6,14},{... | collective-permute-start | bytes 516104 | tf_op jit(solution)/shard_map/ppermute | solution.py:459
  24.1 8.7 %collective-permute-start.2 = (bf16[4,48,384]{2,1,0:T(8,128)(2,1)S(1)}, bf16[4,48,384]{2,1,0:T(8,128)(2,1)S(1)}, u32[]{:S(2)}, u32[]{:S(2)}) collective-permute-start(bf16[4,48,384]{2,1,0:T(8,128)(2,1)S(1)} %get-tuple-element.49), channel_id=1, source_target_pairs={{0,3},{1,2},{2,1},{3,0},{4,7},{5,6},{6,5},{7,4},{8,11},{9,10},{10,... | collective-permute-start | bytes 442376 | tf_op jit(solution)/shard_map/ppermute | solution.py:445
  28.0 10.9 %collective-permute-start.13 = (bf16[1,48,1536]{2,1,0:T(8,128)(2,1)S(1)}, bf16[1,48,1536]{2,1,0:T(8,128)(2,1)S(1)}, u32[]{:S(2)}, u32[]{:S(2)}) collective-permute-start(bf16[1,48,1536]{2,1,0:T(8,128)(2,1)S(1)} %collective-permute-done.6.refs_1_), channel_id=1, source_target_pairs={{0,4},{4,12},{12,8},{8,0},{1,5},{5,13},{13,9},{9,1},{2,6},{6,14},{... | collective-permute-start | bytes 442376 | tf_op jit(solution)/shard_map/ppermute | solution.py:459
  31.5 9.5 %collective-permute-start.8 = (bf16[1,48,1536]{2,1,0:T(8,128)(2,1)S(1)}, bf16[1,48,1536]{2,1,0:T(8,128)(2,1)S(1)}, u32[]{:S(2)}, u32[]{:S(2)}) collective-permute-start(bf16[1,48,1536]{2,1,0:T(8,128)(2,1)S(1)} %collective-permute-done.7.refs_2_), channel_id=1, source_target_pairs={{0,4},{4,12},{12,8},{8,0},{1,5},{5,13},{13,9},{9,1},{2,6},{6,14},{... | collective-permute-start | bytes 442376 | tf_op jit(solution)/shard_map/ppermute | solution.py:459
  31.5 13.5 %collective-permute-start.4 = (bf16[1,48,1536]{2,1,0:T(8,128)(2,1)S(1)}, bf16[1,48,1536]{2,1,0:T(8,128)(2,1)S(1)}, u32[]{:S(2)}, u32[]{:S(2)}) collective-permute-start(bf16[1,48,1536]{2,1,0:T(8,128)(2,1)S(1)} %collective-permute-done.3.refs_1_), channel_id=1, source_target_pairs={{0,4},{4,12},{12,8},{8,0},{1,5},{5,13},{13,9},{9,1},{2,6},{6,14},{... | collective-permute-start | bytes 442376 | tf_op jit(solution)/shard_map/ppermute | solution.py:459
  39.0 8.1 %collective-permute-start.14 = (bf16[1,48,1536]{2,1,0:T(8,128)(2,1)S(1)}, bf16[1,48,1536]{2,1,0:T(8,128)(2,1)S(1)}, u32[]{:S(2)}, u32[]{:S(2)}) collective-permute-start(bf16[1,48,1536]{2,1,0:T(8,128)(2,1)S(1)} %collective-permute-done.13.refs_2_), channel_id=1, source_target_pairs={{0,4},{4,12},{12,8},{8,0},{1,5},{5,13},{13,9},{9,1},{2,6},{6,14},{... | collective-permute-start | bytes 442376 | tf_op jit(solution)/shard_map/ppermute | solution.py:459
  45.0 6.1 %collective-permute-start.12 = (bf16[1,48,1536]{2,1,0:T(8,128)(2,1)S(1)}, bf16[1,48,1536]{2,1,0:T(8,128)(2,1)S(1)}, u32[]{:S(2)}, u32[]{:S(2)}) collective-permute-start(bf16[1,48,1536]{2,1,0:T(8,128)(2,1)S(1)} %collective-permute-done.4.refs_2_), channel_id=1, source_target_pairs={{0,4},{4,12},{12,8},{8,0},{1,5},{5,13},{13,9},{9,1},{2,6},{6,14},{... | collective-permute-start | bytes 442376 | tf_op jit(solution)/shard_map/ppermute | solution.py:459

commit v5 on v4

--- a/solution.py
+++ b/solution.py
@@ -303,17 +303,6 @@
         place = sum(jnp.where(me == m, sources[m][k], 0) for m in range(parts))
         start = pl.multiple_of(place * size, 16)
         dz_ref[pl.ds(start, size), :] = shards[k][:, :width]
-    if not t:
-        total = sum(shard[:, width + i : width + i + 128].astype(F32) for shard in shards for i in (0, 128))
-        lines_ref = refs[3]
-        lines_ref[...] = total
-        share = gain_ref.shape[1] // 128
-        cols = width // 128
-        for i in range(gain_ref.shape[0]):
-            for j in range(share):
-                gain_ref[i : i + 1, j * 128 : (j + 1) * 128] = lines_ref[
-                    pl.ds(i * cols + me * share + j, 1), :
-                ]
     dz = dz_ref[...]
     hidden = out_ref.shape[0]
     block = hidden // 3
@@ -362,8 +351,22 @@
         spill(rows_ref.at[i * cols : (i + 1) * cols], spill_ref.at[i % 2])
         write(spill_ref.at[i % 2], pre_ref.at[:, :, pl.ds(i * block, block)], 3 + i)
 
+    def gain():
+        total = sum(shard[:, width + i : width + i + 128].astype(F32) for shard in shards for i in (0, 128))
+        lines_ref = refs[3]
+        lines_ref[...] = total
+        share = gain_ref.shape[1] // 128
+        cols = width // 128
+        for i in range(gain_ref.shape[0]):
+            for j in range(share):
+                gain_ref[i : i + 1, j * 128 : (j + 1) * 128] = lines_ref[
+                    pl.ds(i * cols + me * share + j, 1), :
+                ]
+
     for i in range(3):
         down(i)
+        if i == 0 and t == 0:
+            gain()
         back(i)
     for k, copy in enumerate(writes):
         if not merge or k != 1:

time: 57.2 us -> 57.2 us (level)
  no operation moved by 1% of the time
where the time goes in v5:
time: 57.2 us; the launch traced here: 57 us
  Pallas kernels  31.6 us (55%)
  starting transfers between devices  21.5 us (38%)
  waiting for transfers between devices  3.04 us (5%)
  between operations  0.89 us (2%)
    ppermute x12, starting transfers between devices, hop(): lax.ppermute(after(last, *others) if others else last, 'dp', ring)  19.7 us
    pallas_call x4, Pallas kernels, token_step(): pl.pallas_call(functools.partial(token_kernel, t, at, parts, merge, sourc...  18.7 us
    pallas_call x2, Pallas kernels, activations(): pl.pallas_call(functools.partial(act_kernel, parts, first, toks), in_spec...  8.55 us
    ppermute x12, waiting for transfers between devices, hop(): lax.ppermute(after(last, *others) if others else last, 'dp', ring)  3.04 us
    pallas_call x1, Pallas kernels, norm(): pl.pallas_call(functools.partial(norm_kernel, pieces, len(chunks)), out_s...  2.98 us
    ppermute x3, starting transfers between devices, swap(): lax.ppermute(v, 'tok', [(p, p ^ k + 1) for p in range(groups)])  1.76 us
    pallas_call x1, Pallas kernels, mix(): pl.pallas_call(functools.partial(mix_kernel, 1 + len(recv)), out_shape=ja...  1.34 us
  transfers between devices with their start and end apart: 15, of which 1 were waited for; matrix products, arithmetic and copies ran while one was open for 0% of the time, Pallas kernels for 40%

profile of v5, /device:TPU:0, one launch (start us, length us, event | category | flops | bytes accessed | tf_op | source)
XLA Modules:
  0.0 57.0 jit_solution(12387289810300642095)
XLA Ops:
  0.6 3.0 %norm.1 = (bf16[1,48,1792]{2,1,0:T(8,128)(2,1)S(1)}, bf16[1,48,1536]{2,1,0:T(8,128)(2,1)S(1)}, bf16[1,48,1536]{2,1,0:T(8,128)(2,1)S(1)}, bf16[1,48,1536]{2,1,0:T...) custom-call(bf16[48,4,1536]{2,1,0:T(4,128)(2,1)} %x_hbm.1, ...), custom_call_target="tpu_custom_call" | custom-call | tf_op jit(solution)/shard_map/norm/pallas_call | solution.py:115
  3.6 3.1 %collective-permute-start.9 = (bf16[1,48,1792]{2,1,0:T(8,128)(2,1)S(1)}, bf16[1,48,1792]{2,1,0:T(8,128)(2,1)S(1)}, u32[]{:S(2)}, u32[]{:S(2)}) collective-permute-start(bf16[1,48,1792]{2,1,0:T(8,128)(2,1)S(1)} %get-tuple-element.51.refs_3_.refs_0_), channel_id=1, source_target_pairs={{0,4},{4,12},{12,8},{8,0},{1,5},{5,13},{13,9},{9,1},{2,6},{6,14},{... | collective-permute-start | bytes 516104 | tf_op jit(solution)/shard_map/ppermute | solution.py:462
  6.7 2.6 %collective-permute-start.5 = (bf16[1,48,1536]{2,1,0:T(8,128)(2,1)S(1)}, bf16[1,48,1536]{2,1,0:T(8,128)(2,1)S(1)}, u32[]{:S(2)}, u32[]{:S(2)}) collective-permute-start(bf16[1,48,1536]{2,1,0:T(8,128)(2,1)S(1)} %get-tuple-element.52.refs_4_.refs_0_), channel_id=1, source_target_pairs={{0,4},{4,12},{12,8},{8,0},{1,5},{5,13},{13,9},{9,1},{2,6},{6,14},{... | collective-permute-start | bytes 442376 | tf_op jit(solution)/shard_map/ppermute | solution.py:462
  9.3 0.4 collective-permute-start.6
  9.7 4.6 %act.2 = (bf16[2,192,1536]{2,1,0:T(8,128)(2,1)S(1)}, f32[2,192,1536]{2,1,0:T(8,128)S(1)}, f32[2,192,1536]{2,1,0:T(8,128)S(1)}, bf16[2,1536,1536]{2,1,0:T(8,128)(...) custom-call(bf16[192,4,1536]{2,1,0:T(4,128)(2,1)} %source.1, f32[8,4,1536]{2,1,0:T(4,128)} %gates_hbm.3, ...), custom_call_target="tpu_custom_call" | custom-call | flops 1 | bytes 1 | tf_op jit(solution)/shard_map/act/pallas_call | solution.py:268
  14.4 0.0 collective-permute-done.9.refs_1_
  14.4 0.1 collective-permute-start.10
  14.5 0.0 collective-permute-start
  14.5 1.7 %collective-permute-start.1 = (bf16[4,48,384]{2,1,0:T(8,128)(2,1)S(1)}, bf16[4,48,384]{2,1,0:T(8,128)(2,1)S(1)}, u32[]{:S(2)}, u32[]{:S(2)}) collective-permute-start(bf16[4,48,384]{2,1,0:T(8,128)(2,1)S(1)} %get-tuple-element.47), channel_id=1, source_target_pairs={{0,2},{1,3},{2,0},{3,1},{4,6},{5,7},{6,4},{7,5},{8,10},{9,11},{10,... | collective-permute-start | bytes 442376 | tf_op jit(solution)/shard_map/ppermute | solution.py:448
  16.3 3.0 %collective-permute-done.6.refs_1_ = bf16[1,48,1536]{2,1,0:T(8,128)(2,1)S(1)} collective-permute-done((bf16[1,48,1536]{2,1,0:T(8,128)(2,1)S(1)}, bf16[1,48,1536]{2,1,0:T(8,128)(2,1)S(1)}, u32[]{:S(2)}, u32[]{:S(2)}) %collective-permute-start.6) | collective-permute-done | bytes 147488 | tf_op jit(solution)/shard_map/ppermute | solution.py:462
  19.2 1.2 %collective-permute-start.7 = (bf16[1,48,1536]{2,1,0:T(8,128)(2,1)S(1)}, bf16[1,48,1536]{2,1,0:T(8,128)(2,1)S(1)}, u32[]{:S(2)}, u32[]{:S(2)}) collective-permute-start(bf16[1,48,1536]{2,1,0:T(8,128)(2,1)S(1)} %collective-permute-done.5.refs_1_), channel_id=1, source_target_pairs={{0,4},{4,12},{12,8},{8,0},{1,5},{5,13},{13,9},{9,1},{2,6},{6,14},{... | collective-permute-start | bytes 442376 | tf_op jit(solution)/shard_map/ppermute | solution.py:462
  20.4 3.4 %collective-permute-start.3 = (bf16[1,48,1536]{2,1,0:T(8,128)(2,1)S(1)}, bf16[1,48,1536]{2,1,0:T(8,128)(2,1)S(1)}, u32[]{:S(2)}, u32[]{:S(2)}) collective-permute-start(bf16[1,48,1536]{2,1,0:T(8,128)(2,1)S(1)} %get-tuple-element.54.refs_6_.refs_0_), channel_id=1, source_target_pairs={{0,4},{4,12},{12,8},{8,0},{1,5},{5,13},{13,9},{9,1},{2,6},{6,14},{... | collective-permute-start | bytes 442376 | tf_op jit(solution)/shard_map/ppermute | solution.py:462
  23.8 0.3 collective-permute-start.11
  24.1 3.9 %act.3 = (bf16[2,192,1536]{2,1,0:T(8,128)(2,1)S(1)}, f32[2,192,1536]{2,1,0:T(8,128)S(1)}, f32[2,192,1536]{2,1,0:T(8,128)S(1)}, bf16[2,1536,1536]{2,1,0:T(8,128)(2,1)S(1)}) custom-call(f32[2,192,1536]{2,1,0:T(8,128)S(1)} %get-tuple-element.66.source, f32[8,4,1536]{2,1,0:T(4,128)} %gates_hbm.3, bf16[8,192]{1,0:T(8,128)(2,1)S(1)} %get-tuple-element.60.refs_8_.pick, ...), custom_call_target="tpu_custom_call" | custom-call | flops 1 | bytes 1 | tf_op jit(solution)/shard_map/act/pallas_call | solution.py:268
  28.0 0.0 collective-permute-done.1.refs_1_
  28.0 3.4 %collective-permute-start.13 = (bf16[1,48,1536]{2,1,0:T(8,128)(2,1)S(1)}, bf16[1,48,1536]{2,1,0:T(8,128)(2,1)S(1)}, u32[]{:S(2)}, u32[]{:S(2)}) collective-permute-start(bf16[1,48,1536]{2,1,0:T(8,128)(2,1)S(1)} %collective-permute-done.6.refs_1_), channel_id=1, source_target_pairs={{0,4},{4,12},{12,8},{8,0},{1,5},{5,13},{13,9},{9,1},{2,6},{6,14},{... | collective-permute-start | bytes 442376 | tf_op jit(solution)/shard_map/ppermute | solution.py:462
  31.5 0.0 collective-permute-done.7.refs_2_
  31.5 0.1 collective-permute-start.8
  31.5 0.0 collective-permute-done.3.refs_1_
  31.5 1.2 %collective-permute-start.4 = (bf16[1,48,1536]{2,1,0:T(8,128)(2,1)S(1)}, bf16[1,48,1536]{2,1,0:T(8,128)(2,1)S(1)}, u32[]{:S(2)}, u32[]{:S(2)}) collective-permute-start(bf16[1,48,1536]{2,1,0:T(8,128)(2,1)S(1)} %collective-permute-done.3.refs_1_), channel_id=1, source_target_pairs={{0,4},{4,12},{12,8},{8,0},{1,5},{5,13},{13,9},{9,1},{2,6},{6,14},{... | collective-permute-start | bytes 442376 | tf_op jit(solution)/shard_map/ppermute | solution.py:462
  32.7 0.0 collective-permute-done.2.refs_2_
  32.7 1.3 %mix.1 = bf16[48,4,1536]{2,1,0:T(4,128)(2,1)} custom-call(bf16[4,48,384]{2,1,0:T(8,128)(2,1)S(1)} %collective-permute-done.refs_0_, bf16[4,48,384]{2,1,0:T(8,128)(2,1)S(1)} %collective-permute-done.1.refs_1_, bf16[4,48,384]{2,1,0:T(8,128)(2,1)S(1)} %collective-permute-done.2.refs_2_, bf16[1,48,1792]{2,1,0:T(8,128)(2,1)S(1)} %get-tuple-element.51.refs_3_.refs_0_, ...), custom_call_target="tpu_custom_call" | custom-call | flops 1 | bytes 1 | tf_op jit(solution)/shard_map/mix/pallas_call | solution.py:162
  34.1 4.9 %token_.4 = (bf16[4,1536,1536]{2,1,0:T(8,128)(2,1)}, f32[12,768,128]{2,1,0:T(8,128)S(1)}, f32[8,1536]{1,0:T(8,128)S(1)}, f32[4,384]{1,0:T(4,128)}) custom-call(bf16[1,48,1792]{2,1,0:T(8,128)(2,1)S(1)} %get-tuple-element.51.refs_3_.refs_0_, bf16[1,48,1792]{2,1,0:T(8,128)(2,1)S(1)} %collective-permute-done.9.refs_1_, ...), custom_call_target="tpu_custom_call" | custom-call | flops 1 | bytes 1 | tf_op jit(solution)/shard_map/token/pallas_call | solution.py:415
  39.0 0.0 collective-permute-done.13.refs_2_
  39.0 2.0 %collective-permute-start.14 = (bf16[1,48,1536]{2,1,0:T(8,128)(2,1)S(1)}, bf16[1,48,1536]{2,1,0:T(8,128)(2,1)S(1)}, u32[]{:S(2)}, u32[]{:S(2)}) collective-permute-start(bf16[1,48,1536]{2,1,0:T(8,128)(2,1)S(1)} %collective-permute-done.13.refs_2_), channel_id=1, source_target_pairs={{0,4},{4,12},{12,8},{8,0},{1,5},{5,13},{13,9},{9,1},{2,6},{6,14},{... | collective-permute-start | bytes 442376 | tf_op jit(solution)/shard_map/ppermute | solution.py:462
  40.9 0.0 collective-permute-done.8.refs_3_
  40.9 4.1 %token_.5 = (bf16[4,1536,1536]{2,1,0:T(8,128)(2,1)}, f32[12,768,128]{2,1,0:T(8,128)S(1)}, f32[8,1536]{1,0:T(8,128)S(1)}) custom-call(bf16[1,48,1536]{2,1,0:T(8,128)(2,1)S(1)} %get-tuple-element.52.refs_4_.refs_0_, bf16[1,48,1536]{2,1,0:T(8,128)(2,1)S(1)} %collective-permute-done.5.refs_1_, ...), custom_call_target="tpu_custom_call", output_to_operand_aliasing={{0}: (9, {}), {1}: (10, {})} | custom-call | flops 1 | bytes 1 | tf_op jit(solution)/shard_map/token/pallas_call | solution.py:415
  45.0 0.0 collective-permute-done.4.refs_2_
  45.0 2.0 %collective-permute-start.12 = (bf16[1,48,1536]{2,1,0:T(8,128)(2,1)S(1)}, bf16[1,48,1536]{2,1,0:T(8,128)(2,1)S(1)}, u32[]{:S(2)}, u32[]{:S(2)}) collective-permute-start(bf16[1,48,1536]{2,1,0:T(8,128)(2,1)S(1)} %collective-permute-done.4.refs_2_), channel_id=1, source_target_pairs={{0,4},{4,12},{12,8},{8,0},{1,5},{5,13},{13,9},{9,1},{2,6},{6,14},{... | collective-permute-start | bytes 442376 | tf_op jit(solution)/shard_map/ppermute | solution.py:462
  47.0 4.1 %token_.6 = (bf16[4,1536,1536]{2,1,0:T(8,128)(2,1)}, f32[12,768,128]{2,1,0:T(8,128)S(1)}, f32[8,1536]{1,0:T(8,128)S(1)}) custom-call(bf16[1,48,1536]{2,1,0:T(8,128)(2,1)S(1)} %get-tuple-element.53.refs_5_.refs_0_, bf16[1,48,1536]{2,1,0:T(8,128)(2,1)S(1)} %collective-permute-done.6.refs_1_, ...), custom_call_target="tpu_custom_call", output_to_operand_aliasing={{0}: (9, {}), {1}: (10, {})} | custom-call | flops 1 | bytes 1 | tf_op jit(solution)/shard_map/token/pallas_call | solution.py:415
  51.1 0.0 collective-permute-done.12.refs_3_
  51.1 5.8 %token_.7 = (bf16[4,1536,1536]{2,1,0:T(8,128)(2,1)}, f32[12,768,128]{2,1,0:T(8,128)S(1)}, f32[8,4,1536]{2,1,0:T(4,128)}, bf16[192,4,1536]{2,1,0:T(4,128)(2,1)}) custom-call(bf16[1,48,1536]{2,1,0:T(8,128)(2,1)S(1)} %get-tuple-element.54.refs_6_.refs_0_, ...), custom_call_target="tpu_custom_call", output_to_operand_aliasing={{0}: (9, {}), {1}: (10, {})} | custom-call | flops 1 | bytes 1 | tf_op jit(solution)/shard_map/token/pallas_call | solution.py:415
  (6 shorter events, 0.0 us)
Async XLA Ops:
  3.6 10.7 %collective-permute-start.9 = (bf16[1,48,1792]{2,1,0:T(8,128)(2,1)S(1)}, bf16[1,48,1792]{2,1,0:T(8,128)(2,1)S(1)}, u32[]{:S(2)}, u32[]{:S(2)}) collective-permute-start(bf16[1,48,1792]{2,1,0:T(8,128)(2,1)S(1)} %get-tuple-element.51.refs_3_.refs_0_), channel_id=1, source_target_pairs={{0,4},{4,12},{12,8},{8,0},{1,5},{5,13},{13,9},{9,1},{2,6},{6,14},{... | collective-permute-start | bytes 516104 | tf_op jit(solution)/shard_map/ppermute | solution.py:462
  6.7 9.6 %collective-permute-start.5 = (bf16[1,48,1536]{2,1,0:T(8,128)(2,1)S(1)}, bf16[1,48,1536]{2,1,0:T(8,128)(2,1)S(1)}, u32[]{:S(2)}, u32[]{:S(2)}) collective-permute-start(bf16[1,48,1536]{2,1,0:T(8,128)(2,1)S(1)} %get-tuple-element.52.refs_4_.refs_0_), channel_id=1, source_target_pairs={{0,4},{4,12},{12,8},{8,0},{1,5},{5,13},{13,9},{9,1},{2,6},{6,14},{... | collective-permute-start | bytes 442376 | tf_op jit(solution)/shard_map/ppermute | solution.py:462
  9.3 9.9 %collective-permute-start.6 = (bf16[1,48,1536]{2,1,0:T(8,128)(2,1)S(1)}, bf16[1,48,1536]{2,1,0:T(8,128)(2,1)S(1)}, u32[]{:S(2)}, u32[]{:S(2)}) collective-permute-start(bf16[1,48,1536]{2,1,0:T(8,128)(2,1)S(1)} %get-tuple-element.53.refs_5_.refs_0_), channel_id=1, source_target_pairs={{0,4},{4,12},{12,8},{8,0},{1,5},{5,13},{13,9},{9,1},{2,6},{6,14},{... | collective-permute-start | bytes 442376 | tf_op jit(solution)/shard_map/ppermute | solution.py:462
  14.4 9.4 %collective-permute-start.10 = (bf16[1,48,1792]{2,1,0:T(8,128)(2,1)S(1)}, bf16[1,48,1792]{2,1,0:T(8,128)(2,1)S(1)}, u32[]{:S(2)}, u32[]{:S(2)}) collective-permute-start(bf16[1,48,1792]{2,1,0:T(8,128)(2,1)S(1)} %collective-permute-done.9.refs_1_), channel_id=1, source_target_pairs={{0,4},{4,12},{12,8},{8,0},{1,5},{5,13},{13,9},{9,1},{2,6},{6,14},{... | collective-permute-start | bytes 516104 | tf_op jit(solution)/shard_map/ppermute | solution.py:462
  14.5 9.6 %collective-permute-start = (bf16[4,48,384]{2,1,0:T(8,128)(2,1)S(1)}, bf16[4,48,384]{2,1,0:T(8,128)(2,1)S(1)}, u32[]{:S(2)}, u32[]{:S(2)}) collective-permute-start(bf16[4,48,384]{2,1,0:T(8,128)(2,1)S(1)} %get-tuple-element.44), channel_id=1, source_target_pairs={{0,1},{1,0},{2,3},{3,2},{4,5},{5,4},{6,7},{7,6},{8,9},{9,8},{10,11... | collective-permute-start | bytes 442376 | tf_op jit(solution)/shard_map/ppermute | solution.py:448
  14.5 13.5 %collective-permute-start.1 = (bf16[4,48,384]{2,1,0:T(8,128)(2,1)S(1)}, bf16[4,48,384]{2,1,0:T(8,128)(2,1)S(1)}, u32[]{:S(2)}, u32[]{:S(2)}) collective-permute-start(bf16[4,48,384]{2,1,0:T(8,128)(2,1)S(1)} %get-tuple-element.47), channel_id=1, source_target_pairs={{0,2},{1,3},{2,0},{3,1},{4,6},{5,7},{6,4},{7,5},{8,10},{9,11},{10,... | collective-permute-start | bytes 442376 | tf_op jit(solution)/shard_map/ppermute | solution.py:448
  19.2 12.2 %collective-permute-start.7 = (bf16[1,48,1536]{2,1,0:T(8,128)(2,1)S(1)}, bf16[1,48,1536]{2,1,0:T(8,128)(2,1)S(1)}, u32[]{:S(2)}, u32[]{:S(2)}) collective-permute-start(bf16[1,48,1536]{2,1,0:T(8,128)(2,1)S(1)} %collective-permute-done.5.refs_1_), channel_id=1, source_target_pairs={{0,4},{4,12},{12,8},{8,0},{1,5},{5,13},{13,9},{9,1},{2,6},{6,14},{... | collective-permute-start | bytes 442376 | tf_op jit(solution)/shard_map/ppermute | solution.py:462
  20.4 11.2 %collective-permute-start.3 = (bf16[1,48,1536]{2,1,0:T(8,128)(2,1)S(1)}, bf16[1,48,1536]{2,1,0:T(8,128)(2,1)S(1)}, u32[]{:S(2)}, u32[]{:S(2)}) collective-permute-start(bf16[1,48,1536]{2,1,0:T(8,128)(2,1)S(1)} %get-tuple-element.54.refs_6_.refs_0_), channel_id=1, source_target_pairs={{0,4},{4,12},{12,8},{8,0},{1,5},{5,13},{13,9},{9,1},{2,6},{6,14},{... | collective-permute-start | bytes 442376 | tf_op jit(solution)/shard_map/ppermute | solution.py:462
  23.8 10.3 %collective-permute-start.11 = (bf16[1,48,1792]{2,1,0:T(8,128)(2,1)S(1)}, bf16[1,48,1792]{2,1,0:T(8,128)(2,1)S(1)}, u32[]{:S(2)}, u32[]{:S(2)}) collective-permute-start(bf16[1,48,1792]{2,1,0:T(8,128)(2,1)S(1)} %collective-permute-done.10.refs_2_), channel_id=1, source_target_pairs={{0,4},{4,12},{12,8},{8,0},{1,5},{5,13},{13,9},{9,1},{2,6},{6,14},{... | collective-permute-start | bytes 516104 | tf_op jit(solution)/shard_map/ppermute | solution.py:462
  24.1 8.7 %collective-permute-start.2 = (bf16[4,48,384]{2,1,0:T(8,128)(2,1)S(1)}, bf16[4,48,384]{2,1,0:T(8,128)(2,1)S(1)}, u32[]{:S(2)}, u32[]{:S(2)}) collective-permute-start(bf16[4,48,384]{2,1,0:T(8,128)(2,1)S(1)} %get-tuple-element.49), channel_id=1, source_target_pairs={{0,3},{1,2},{2,1},{3,0},{4,7},{5,6},{6,5},{7,4},{8,11},{9,10},{10,... | collective-permute-start | bytes 442376 | tf_op jit(solution)/shard_map/ppermute | solution.py:448
  28.0 10.9 %collective-permute-start.13 = (bf16[1,48,1536]{2,1,0:T(8,128)(2,1)S(1)}, bf16[1,48,1536]{2,1,0:T(8,128)(2,1)S(1)}, u32[]{:S(2)}, u32[]{:S(2)}) collective-permute-start(bf16[1,48,1536]{2,1,0:T(8,128)(2,1)S(1)} %collective-permute-done.6.refs_1_), channel_id=1, source_target_pairs={{0,4},{4,12},{12,8},{8,0},{1,5},{5,13},{13,9},{9,1},{2,6},{6,14},{... | collective-permute-start | bytes 442376 | tf_op jit(solution)/shard_map/ppermute | solution.py:462
  31.5 9.5 %collective-permute-start.8 = (bf16[1,48,1536]{2,1,0:T(8,128)(2,1)S(1)}, bf16[1,48,1536]{2,1,0:T(8,128)(2,1)S(1)}, u32[]{:S(2)}, u32[]{:S(2)}) collective-permute-start(bf16[1,48,1536]{2,1,0:T(8,128)(2,1)S(1)} %collective-permute-done.7.refs_2_), channel_id=1, source_target_pairs={{0,4},{4,12},{12,8},{8,0},{1,5},{5,13},{13,9},{9,1},{2,6},{6,14},{... | collective-permute-start | bytes 442376 | tf_op jit(solution)/shard_map/ppermute | solution.py:462
  31.5 13.5 %collective-permute-start.4 = (bf16[1,48,1536]{2,1,0:T(8,128)(2,1)S(1)}, bf16[1,48,1536]{2,1,0:T(8,128)(2,1)S(1)}, u32[]{:S(2)}, u32[]{:S(2)}) collective-permute-start(bf16[1,48,1536]{2,1,0:T(8,128)(2,1)S(1)} %collective-permute-done.3.refs_1_), channel_id=1, source_target_pairs={{0,4},{4,12},{12,8},{8,0},{1,5},{5,13},{13,9},{9,1},{2,6},{6,14},{... | collective-permute-start | bytes 442376 | tf_op jit(solution)/shard_map/ppermute | solution.py:462
  39.0 8.1 %collective-permute-start.14 = (bf16[1,48,1536]{2,1,0:T(8,128)(2,1)S(1)}, bf16[1,48,1536]{2,1,0:T(8,128)(2,1)S(1)}, u32[]{:S(2)}, u32[]{:S(2)}) collective-permute-start(bf16[1,48,1536]{2,1,0:T(8,128)(2,1)S(1)} %collective-permute-done.13.refs_2_), channel_id=1, source_target_pairs={{0,4},{4,12},{12,8},{8,0},{1,5},{5,13},{13,9},{9,1},{2,6},{6,14},{... | collective-permute-start | bytes 442376 | tf_op jit(solution)/shard_map/ppermute | solution.py:462
  45.0 6.1 %collective-permute-start.12 = (bf16[1,48,1536]{2,1,0:T(8,128)(2,1)S(1)}, bf16[1,48,1536]{2,1,0:T(8,128)(2,1)S(1)}, u32[]{:S(2)}, u32[]{:S(2)}) collective-permute-start(bf16[1,48,1536]{2,1,0:T(8,128)(2,1)S(1)} %collective-permute-done.4.refs_2_), channel_id=1, source_target_pairs={{0,4},{4,12},{12,8},{8,0},{1,5},{5,13},{13,9},{9,1},{2,6},{6,14},{... | collective-permute-start | bytes 442376 | tf_op jit(solution)/shard_map/ppermute | solution.py:462
